TPU v7x, 32 devices: a whole 2x2x4 slice. The times are simulated.
32 devices in a mesh: dp: 8 (over y, x, core), vocab: 4 (over z).
Axes of the slice: x: 2, y: 2, z: 4, core: 2. Of those that a mesh axis runs over, the one named last changes fastest.
Arguments:
- code_ids: int32 [96, 256], P(('dp', 'vocab')), may hold values from 0 to 1023
- masked: int32 [96, 256], P(('dp', 'vocab')), may hold values from 0 to 1, as said below
- labels: int32 [96], P(('dp', 'vocab')), may hold values from 0 to 999
- dropped: int32 [96], P(('dp', 'vocab')), may hold values 0 or 1
- owners: int32 [24], replicated, may hold values from 0 to 7, as said below
- step_count: int32 [1], replicated, may hold values from 2 to 20
- master_block_weight: float32 [32, 768, 768], P('dp'), may hold values from -0.21875 to 0.21875
- matrix_first_moment: float32 [32, 768, 768], P('dp'), may hold values from -0.00061035156 to 0.00061035156
- matrix_second_moment: float32 [32, 768, 768], P('dp'), may hold values from 5.859375e-09 to 2.4820963e-08
- embed_weight: float32 [1024, 768], P('vocab'), may hold values from -0.875 to 0.875
- embed_first: float32 [1024, 768], P('vocab'), may hold values from -0.00061035156 to 0.00061035156
- embed_second: float32 [1024, 768], P('vocab'), may hold values from 5.859375e-09 to 2.4820963e-08
- extra_weight: float32 [1259, 768], replicated, may hold values from -6 to 6
- extra_first: float32 [1259, 768], replicated, may hold values from -0.00061035156 to 0.00061035156
- extra_second: float32 [1259, 768], replicated, may hold values from 5.859375e-09 to 2.4820963e-08
- norm_weight: float32 [10, 768], replicated, may hold values from -1.5 to 1.5
- norm_first: float32 [10, 768], replicated, may hold values from -0.00061035156 to 0.00061035156
- norm_second: float32 [10, 768], replicated, may hold values from 5.859375e-09 to 2.4820963e-08
- bias_weight: float32 [1024], replicated, may hold values from -6 to 6
- bias_first: float32 [1024], replicated, may hold values from -0.00061035156 to 0.00061035156
- bias_second: float32 [1024], replicated, may hold values from 5.859375e-09 to 2.4820963e-08
Outputs:
- step_loss: float32 [], replicated
- new_block_weight: float32 [32, 768, 768], P('dp')
- new_block_first: float32 [32, 768, 768], P('dp')
- new_block_second: float32 [32, 768, 768], P('dp')
- new_embed_weight: float32 [1024, 768], P('vocab')
- new_embed_first: float32 [1024, 768], P('vocab')
- new_embed_second: float32 [1024, 768], P('vocab')
- new_extra_weight: float32 [1259, 768], replicated
- new_extra_first: float32 [1259, 768], replicated
- new_extra_second: float32 [1259, 768], replicated
- new_norm_weight: float32 [10, 768], replicated
- new_norm_first: float32 [10, 768], replicated
- new_norm_second: float32 [10, 768], replicated
- new_bias_weight: float32 [1024], replicated
- new_bias_first: float32 [1024], replicated
- new_bias_second: float32 [1024], replicated
Inputs may be any that keep to these rules, and one draw needn't show every extreme that they name: Every image has 1 to 256 masked codes. `owners`: no owner holds more than 4 matrices, and some owner holds exactly 4.
All inputs are finite; a program needn't handle non-finite values. No bound on the sum of `dropped` on one device may be relied on, other than what follows from the above.
Results may differ from a plain program's by a relative error of at most 0.0096.
Values may be sent and summed in bfloat16 or wider, within the bound.
A program may use at most 384 MiB of HBM per device.

v0:
```python
import math

import jax
import jax.numpy as jnp
from jax import lax
from jax.sharding import PartitionSpec as P

MODEL_WIDTH = 768
HEADS = 8
HEAD_DIM = 96
FF = 3072
CODES = 1024
CLASSES = 1000
IMAGE_TOKENS = 256
LAYERS = 2
BLOCKS = 24


NORM_EPS = 1e-05
BETA_ONE = 0.9
BETA_TWO = 0.96
ADAM_EPS = 1e-08
DECAY = 0.045


def norm_rows(inputs, norm_gain, norm_shift):
    row_mean = jnp.mean(inputs, -1, keepdims=True)
    centred = inputs - row_mean
    spread = jnp.mean(centred * centred, -1, keepdims=True)
    return centred * lax.rsqrt(spread + NORM_EPS) * norm_gain + norm_shift


def exact_gelu(inputs):
    return jax.nn.gelu(inputs, approximate=False)


def split_heads(inputs, images):
    return inputs.reshape(images, -1, HEADS, HEAD_DIM)


def attention_scores(queries, key_heads):
    return jnp.einsum(
        "bqhd,bkhd->bhqk", queries, key_heads, preferred_element_type=jnp.float32
    ) * HEAD_DIM ** (-0.5)


def adam_update(weight, moment_one, moment_two, gradient, step_rate, step_float):
    moment_one = BETA_ONE * moment_one + (1.0 - BETA_ONE) * gradient
    moment_two = BETA_TWO * moment_two + (1.0 - BETA_TWO) * gradient * gradient
    fix_one = 1.0 - BETA_ONE**step_float
    fix_two = 1.0 - BETA_TWO**step_float
    weight = weight - step_rate * (
        moment_one / fix_one / (jnp.sqrt(moment_two / fix_two) + ADAM_EPS) + DECAY * weight
    )
    return (weight, moment_one, moment_two)


def layer_forward(stream, layer_weights, norm_gains, images):
    pieces = FF // MODEL_WIDTH
    row_count = stream.shape[0]
    attn_in = norm_rows(stream, norm_gains[0], norm_gains[1]).astype(jnp.bfloat16)
    triple = jnp.einsum(
        "td,jde->jte", attn_in, layer_weights[0:3], preferred_element_type=jnp.float32
    ).astype(jnp.bfloat16)
    scores = attention_scores(split_heads(triple[0], images), split_heads(triple[1], images))
    row_top = jnp.max(scores, -1, keepdims=True)
    expo = jnp.exp(scores - row_top)
    row_total = jnp.sum(expo, -1, keepdims=True)
    probs_low = (expo / row_total).astype(jnp.bfloat16)
    log_total = row_top + jnp.log(row_total)
    attended = (
        jnp.einsum(
            "bhqk,bkhd->bqhd",
            probs_low,
            split_heads(triple[2], images),
            preferred_element_type=jnp.float32,
        )
        .reshape(row_count, MODEL_WIDTH)
        .astype(jnp.bfloat16)
    )
    middle = stream + jnp.dot(attended, layer_weights[3], preferred_element_type=jnp.float32)
    mlp_in = norm_rows(middle, norm_gains[2], norm_gains[3]).astype(jnp.bfloat16)
    up_proj = jnp.einsum(
        "td,jde->tje", mlp_in, layer_weights[4 : 4 + pieces], preferred_element_type=jnp.float32
    ).reshape(row_count, FF)
    hidden = exact_gelu(up_proj).astype(jnp.bfloat16)
    down_out = jnp.einsum(
        "tjd,jde->te",
        hidden.reshape(row_count, pieces, MODEL_WIDTH),
        layer_weights[4 + pieces : 4 + 2 * pieces],
        preferred_element_type=jnp.float32,
    )
    return (
        middle + down_out,
        (stream, attn_in, triple, log_total, attended, middle, mlp_in, up_proj, hidden),
    )


def layer_backward(grad_out, layer_weights, norm_gains, saved_values, images):
    stream, attn_in, triple, log_total, attended, middle, mlp_in, up_proj, hidden = saved_values
    pieces = FF // MODEL_WIDTH
    row_count = stream.shape[0]
    branch = grad_out.astype(jnp.bfloat16)
    grad_hidden = jnp.einsum(
        "te,jde->tjd",
        branch,
        layer_weights[4 + pieces : 4 + 2 * pieces],
        preferred_element_type=jnp.float32,
    ).reshape(row_count, FF)
    grad_down = jnp.einsum(
        "tjd,te->jde",
        hidden.reshape(row_count, pieces, MODEL_WIDTH),
        branch,
        preferred_element_type=jnp.float32,
    )
    grad_upper = (
        jax.vjp(exact_gelu, up_proj)[1](grad_hidden)[0]
        .astype(jnp.bfloat16)
        .reshape(row_count, pieces, MODEL_WIDTH)
    )
    grad_up = jnp.einsum("td,tje->jde", mlp_in, grad_upper, preferred_element_type=jnp.float32)
    grad_mlp_in = jnp.einsum(
        "tje,jde->td", grad_upper, layer_weights[4 : 4 + pieces], preferred_element_type=jnp.float32
    )
    grad_mid_norm, grad_gain_two, grad_shift_two = jax.vjp(
        norm_rows, middle, norm_gains[2], norm_gains[3]
    )[1](grad_mlp_in)
    grad_middle = grad_out + grad_mid_norm
    branch = grad_middle.astype(jnp.bfloat16)
    grad_out_proj = jnp.einsum("td,te->de", attended, branch, preferred_element_type=jnp.float32)
    grad_attended = split_heads(
        jnp.einsum(
            "te,de->td", branch, layer_weights[3], preferred_element_type=jnp.float32
        ).astype(jnp.bfloat16),
        images,
    )
    queries = split_heads(triple[0], images)
    key_heads = split_heads(triple[1], images)
    value_heads = split_heads(triple[2], images)
    attn_probs = jnp.exp(attention_scores(queries, key_heads) - log_total)
    grad_probs = jnp.einsum(
        "bqhd,bkhd->bhqk", grad_attended, value_heads, preferred_element_type=jnp.float32
    )
    grad_scores = (
        attn_probs * (grad_probs - jnp.sum(attn_probs * grad_probs, -1, keepdims=True))
    ).astype(jnp.bfloat16)
    score_scale = HEAD_DIM ** (-0.5)
    grad_query = (
        jnp.einsum("bhqk,bkhd->bqhd", grad_scores, key_heads, preferred_element_type=jnp.float32)
        * score_scale
    )
    grad_keys = (
        jnp.einsum("bhqk,bqhd->bkhd", grad_scores, queries, preferred_element_type=jnp.float32)
        * score_scale
    )
    grad_values = jnp.einsum(
        "bhqk,bqhd->bkhd",
        attn_probs.astype(jnp.bfloat16),
        grad_attended,
        preferred_element_type=jnp.float32,
    )
    grad_triple = (
        jnp.stack([grad_query, grad_keys, grad_values])
        .reshape(3, row_count, MODEL_WIDTH)
        .astype(jnp.bfloat16)
    )
    grad_qkv = jnp.einsum("td,jte->jde", attn_in, grad_triple, preferred_element_type=jnp.float32)
    grad_attn_in = jnp.einsum(
        "jte,jde->td", grad_triple, layer_weights[0:3], preferred_element_type=jnp.float32
    )
    grad_in_norm, grad_gain_one, grad_shift_one = jax.vjp(
        norm_rows, stream, norm_gains[0], norm_gains[1]
    )[1](grad_attn_in)
    gradients = jnp.concatenate([grad_qkv, grad_out_proj[None], grad_up, grad_down], axis=0)
    norm_grads = jnp.stack([grad_gain_one, grad_shift_one, grad_gain_two, grad_shift_two])
    return (grad_middle + grad_in_norm, gradients, norm_grads)


def on_device(
    code_ids,
    masked,
    labels,
    dropped,
    owners,
    step_count,
    master_block_weight,
    matrix_first_moment,
    matrix_second_moment,
    embed_weight,
    embed_first,
    embed_second,
    extra_weight,
    extra_first,
    extra_second,
    norm_weight,
    norm_first,
    norm_second,
    bias_weight,
    bias_first,
    bias_second,
):
    images = code_ids.shape[0]
    seq_len = IMAGE_TOKENS + 1
    slot_count = master_block_weight.shape[0]
    block_count = owners.shape[0]
    per_layer = BLOCKS // LAYERS
    block_index = jnp.arange(block_count)
    same_owner = (owners[None, :] == owners[:, None]) & (
        block_index[None, :] < block_index[:, None]
    )
    owner_rank = jnp.sum(same_owner.astype(jnp.int32), axis=1)
    slot_of = owners * slot_count + owner_rank
    slot_index = jnp.arange(slot_count * lax.axis_size("dp"))
    slot_match = slot_of[None, :] == slot_index[:, None]
    filled = jnp.any(slot_match, axis=1)
    block_of = jnp.sum(jnp.where(slot_match, block_index[None, :], 0), axis=1)
    gathered = lax.all_gather(master_block_weight.astype(jnp.bfloat16), "dp", axis=0, tiled=True)
    all_weights = jnp.take(gathered, slot_of, axis=0)
    local_table = embed_weight.astype(jnp.bfloat16)
    code_table = lax.all_gather(local_table, "vocab", axis=0, tiled=True)
    mask_float = masked.astype(jnp.float32)
    masked_total = lax.psum(jnp.sum(mask_float), ("dp", "vocab"))
    inverse = 1.0 / masked_total
    classes = jnp.where(dropped == 1, CLASSES, labels)
    code_rows = jnp.where(
        mask_float[..., None] > 0,
        extra_weight[IMAGE_TOKENS + 1],
        math.sqrt(MODEL_WIDTH) * jnp.take(code_table, code_ids, axis=0).astype(jnp.float32),
    )
    class_rows = jnp.take(extra_weight, IMAGE_TOKENS + 2 + classes, axis=0)
    stream = (
        jnp.concatenate([class_rows[:, None], code_rows], axis=1) + extra_weight[:seq_len]
    ).reshape(images * seq_len, MODEL_WIDTH)
    saved_layers = []
    for layer_index in range(LAYERS):
        stream, saved_values = layer_forward(
            stream,
            all_weights[per_layer * layer_index : per_layer * (layer_index + 1)],
            norm_weight[4 * layer_index : 4 * layer_index + 4],
            images,
        )
        saved_layers.append(saved_values)
    final_gain = norm_weight[4 * LAYERS]
    final_shift = norm_weight[4 * LAYERS + 1]
    final_rows = norm_rows(stream, final_gain, final_shift)
    own_rows = images * IMAGE_TOKENS
    code_final = (
        final_rows.reshape(images, seq_len, MODEL_WIDTH)[:, 1:]
        .reshape(own_rows, MODEL_WIDTH)
        .astype(jnp.bfloat16)
    )
    flat_mask = mask_float.reshape(own_rows)
    group_rows, group_mask = (
        lax.all_gather(code_final, "vocab", axis=0, tiled=True),
        lax.all_gather(flat_mask.astype(jnp.bfloat16), "vocab", axis=0, tiled=True),
    )
    shard_codes = local_table.shape[0]
    vocab_index = lax.axis_index("vocab")
    local_bias = lax.dynamic_slice_in_dim(bias_weight, vocab_index * shard_codes, shard_codes)
    logits = (
        jnp.einsum("td,cd->tc", group_rows, local_table, preferred_element_type=jnp.float32)
        + local_bias
    )
    row_top = jnp.max(logits, axis=1)
    row_total = jnp.sum(jnp.exp(logits - row_top[:, None]), axis=1)
    group_top = lax.pmax(row_top, "vocab")
    group_total = lax.psum(row_total * jnp.exp(row_top - group_top), "vocab")
    log_total = group_top + jnp.log(group_total)
    row_weight = group_mask.astype(jnp.float32) * inverse
    weighted = jnp.exp(logits - log_total[:, None]) * row_weight[:, None]
    grad_logits = weighted.astype(jnp.bfloat16)
    flat_codes = code_ids.reshape(own_rows)
    target_rows = jnp.take(code_table, flat_codes, axis=0)
    own_weight = flat_mask * inverse
    target_logit = (
        jnp.sum(code_final.astype(jnp.float32) * target_rows.astype(jnp.float32), axis=1)
        + bias_weight[flat_codes]
    )
    own_log_total = lax.dynamic_slice_in_dim(log_total, vocab_index * own_rows, own_rows)
    loss_part = jnp.sum(own_weight * (own_log_total - target_logit))
    grad_code = lax.psum_scatter(
        jnp.dot(grad_logits, local_table, preferred_element_type=jnp.float32).astype(jnp.bfloat16),
        "vocab",
        scatter_dimension=0,
        tiled=True,
    ).astype(jnp.float32)
    grad_code = grad_code - own_weight[:, None] * target_rows.astype(jnp.float32)
    head_table = jnp.einsum(
        "tc,td->cd", grad_logits, group_rows, preferred_element_type=jnp.float32
    )
    head_bias = jnp.sum(weighted, axis=0)
    grad_final = jnp.concatenate(
        [
            jnp.zeros((images, 1, MODEL_WIDTH), jnp.float32),
            grad_code.reshape(images, IMAGE_TOKENS, MODEL_WIDTH),
        ],
        axis=1,
    ).reshape(images * seq_len, MODEL_WIDTH)
    grad_stream, grad_gain, grad_shift = jax.vjp(norm_rows, stream, final_gain, final_shift)[1](
        grad_final
    )
    layer_grads = []
    gain_grads = []
    for layer_index in reversed(range(LAYERS)):
        grad_stream, block_grads, norm_grads = layer_backward(
            grad_stream,
            all_weights[per_layer * layer_index : per_layer * (layer_index + 1)],
            norm_weight[4 * layer_index : 4 * layer_index + 4],
            saved_layers[layer_index],
            images,
        )
        layer_grads.insert(0, block_grads)
        gain_grads.insert(0, norm_grads)
    all_grads = jnp.concatenate(layer_grads, axis=0)
    norm_grad = jnp.concatenate(gain_grads + [jnp.stack([grad_gain, grad_shift])], axis=0)
    token_low = lax.optimization_barrier(grad_stream.astype(jnp.bfloat16)).reshape(
        images, seq_len, MODEL_WIDTH
    )
    token_grad = token_low.astype(jnp.float32)
    position_grad = jnp.sum(grad_stream.reshape(images, seq_len, MODEL_WIDTH), axis=0)
    mask_grad = jnp.sum(mask_float[..., None] * token_grad[:, 1:], axis=(0, 1))
    class_hot = (classes[:, None] == jnp.arange(CLASSES + 1)[None, :]).astype(jnp.bfloat16)
    class_grad = jnp.dot(class_hot.T, token_low[:, 0], preferred_element_type=jnp.float32)
    extra_grad = jnp.concatenate([position_grad, mask_grad[None], class_grad], axis=0)
    code_hot = (flat_codes[:, None] == jnp.arange(CODES)[None, :]).astype(jnp.bfloat16)
    kept_hot = code_hot * (1.0 - flat_mask)[:, None].astype(jnp.bfloat16)
    masked_hot = code_hot * flat_mask[:, None].astype(jnp.bfloat16)
    input_term = jnp.dot(
        kept_hot.T,
        token_low[:, 1:].reshape(own_rows, MODEL_WIDTH),
        preferred_element_type=jnp.float32,
    )
    target_term = jnp.dot(masked_hot.T, code_final, preferred_element_type=jnp.float32)
    table_term = math.sqrt(MODEL_WIDTH) * input_term - inverse * target_term
    table_piece = (
        lax.psum_scatter(
            table_term.astype(jnp.bfloat16), "vocab", scatter_dimension=0, tiled=True
        ).astype(jnp.float32)
        + head_table
    )
    table_grad = lax.psum(table_piece, "dp")
    placed_bias = lax.dynamic_update_slice_in_dim(
        jnp.zeros((CODES,), jnp.float32), head_bias, vocab_index * shard_codes, 0
    )
    bias_grad = placed_bias - inverse * jnp.sum(masked_hot.astype(jnp.float32), axis=0)
    step_loss, extra_grad, norm_grad, bias_grad = lax.psum(
        (loss_part, extra_grad, norm_grad, bias_grad), ("dp", "vocab")
    )
    owned = lax.psum_scatter(
        jnp.where(filled[:, None, None], jnp.take(all_grads, block_of, axis=0), 0.0).astype(
            jnp.bfloat16
        ),
        "dp",
        scatter_dimension=0,
        tiled=True,
    ).astype(jnp.float32)
    owned = lax.psum(owned, "vocab")
    own_filled = lax.dynamic_slice_in_dim(filled, lax.axis_index("dp") * slot_count, slot_count)[
        :, None, None
    ]
    step_float = step_count[0].astype(jnp.float32)
    block_new = adam_update(
        master_block_weight, matrix_first_moment, matrix_second_moment, owned, 0.03, step_float
    )
    table_new = adam_update(embed_weight, embed_first, embed_second, table_grad, 0.05, step_float)
    extra_new = adam_update(extra_weight, extra_first, extra_second, extra_grad, 0.5, step_float)
    norm_new = adam_update(norm_weight, norm_first, norm_second, norm_grad, 0.5, step_float)
    bias_new = adam_update(bias_weight, bias_first, bias_second, bias_grad, 0.3, step_float)
    return (
        step_loss,
        jnp.where(own_filled, block_new[0], 0.0),
        jnp.where(own_filled, block_new[1], 0.0),
        jnp.where(own_filled, block_new[2], 0.0),
        table_new[0],
        table_new[1],
        table_new[2],
        extra_new[0],
        extra_new[1],
        extra_new[2],
        norm_new[0],
        norm_new[1],
        norm_new[2],
        bias_new[0],
        bias_new[1],
        bias_new[2],
    )


def solution(mesh):
    placed = (
        P(("dp", "vocab"), None),
        P(("dp", "vocab"), None),
        P(("dp", "vocab")),
        P(("dp", "vocab")),
        P(),
        P(),
        P("dp", None, None),
        P("dp", None, None),
        P("dp", None, None),
        P("vocab", None),
        P("vocab", None),
        P("vocab", None),
        P(),
        P(),
        P(),
        P(),
        P(),
        P(),
        P(),
        P(),
        P(),
    )
    return jax.shard_map(
        on_device,
        mesh=mesh,
        in_specs=placed,
        out_specs=(
            P(),
            P("dp", None, None),
            P("dp", None, None),
            P("dp", None, None),
            P("vocab", None),
            P("vocab", None),
            P("vocab", None),
            P(),
            P(),
            P(),
            P(),
            P(),
            P(),
            P(),
            P(),
            P(),
        ),
        check_vma=False,
    )
```

profile of v0, /device:TPU:0, one launch (start us, length us, event | category | flops | bytes accessed | tf_op | source)
XLA Modules:
  0.0 1720.1 jit_solution(17351287396638025507)
XLA Ops:
  22.8 27.2 %all-gather.5.cloned.1.call-done = bf16[1024,768]{1,0:T(8,128)(2,1)} async-done(((bf16[256,768]{1,0:T(8,128)(2,1)}), bf16[1024,768]{1,0:T(8,128)(2,1)}) %all-gather.5.cloned.1.call-update) | async-done | bytes 1572880 | tf_op jit(solution)/shard_map/all_gather | solution.py:220
  68.3 162.7 %all-gather.7.cloned.1.call-done = bf16[32,768,768]{2,1,0:T(8,128)(2,1)} async-done(((bf16[4,768,768]{2,1,0:T(8,128)(2,1)}), bf16[32,768,768]{2,1,0:T(8,128)(2,1)}) %all-gather.7.cloned.1.call-update) | async-done | bytes 37748752 | tf_op jit(solution)/shard_map/all_gather | solution.py:217
  230.9 19.0 %gather_fusion.2 = bf16[24,768,768]{2,1,0:T(8,128)(2,1)} fusion(bf16[32,768,768]{2,1,0:T(8,128)(2,1)} %all-gather.7.cloned.1.call-done, s32[1024]{0:T(1024)S(1)} %pad_clamp_fusion.2), kind=kCustom, calls=%fused_computation.2 | custom fusion | bytes 56623200 | tf_op jit(solution)/shard_map/jit(_take)/gather | solution.py:218
  250.0 19.8 %broadcast_select_fusion = bf16[24,768,768]{2,1,0:T(8,128)(2,1)} fusion(bf16[24,768,768]{2,1,0:T(8,128)(2,1)} %gather_fusion.2, pred[24]{0:T(512)(128)(4,1)S(1)} %get-tuple-element.143), kind=kLoop, calls=%fused_computation.7 | loop fusion | flops 14155776 | bytes 56623128 | tf_op jit(solution)/shard_map/jit(_take)/select_n | solution.py:218
  313.1 22.6 %multiply_convert_fusion.3 = (bf16[771,4,768]{2,0,1:T(8,128)(2,1)S(1)}, f32[771,4,768]{2,0,1:T(8,128)}) fusion(f32[771,4,768]{2,0,1:T(8,128)S(1)} %get-tuple-element.167, u8[771,768]{1,0:T(8,128)(4,1)S(1)} %get-tuple-element.83, u8[771,768]{1,0:T(8,128)(4,1)S(1)} %get-tuple-element.82), kind=kLoop, calls=%fused_computation.47 | loop fusion | flops 165795840 | bytes 24869376 | tf_op jit(solution)/shard_map/convert_element_type | solution.py:86
  389.7 22.9 %multiply_convert_fusion.2 = (bf16[771,4,768]{2,0,1:T(8,128)(2,1)S(1)}, f32[771,4,768]{2,0,1:T(8,128)}) fusion(f32[771,4,768]{2,0,1:T(8,128)S(1)} %get-tuple-element.174, u8[771,768]{1,0:T(8,128)(4,1)S(1)} %get-tuple-element.81, u8[771,768]{1,0:T(8,128)(4,1)S(1)} %get-tuple-element.80), kind=kLoop, calls=%fused_computation.34 | loop fusion | flops 165795840 | bytes 24869376 | tf_op jit(solution)/shard_map/convert_element_type | solution.py:86
  430.1 43.4 %psum.56 = f32[]{:T(128)} all-reduce(f32[]{:T(128)} %get-tuple-element.162), channel_id=1, replica_groups=mesh['dp'=8,'vocab'=4] {'dp','vocab'}, use_global_device_ids=true, to_apply=%region_1.0 | all-reduce | flops 1 | bytes 8 | tf_op jit(solution)/shard_map/psum | solution.py:222
  476.1 14.2 all-gather
  490.3 29.2 %all-gather.9.cloned.1.call-done = bf16[3072,768]{1,0:T(8,128)(2,1)} async-done(((bf16[768,768]{1,0:T(8,128)(2,1)}), bf16[3072,768]{1,0:T(8,128)(2,1)}) %all-gather.9.cloned.1.call-update) | async-done | bytes 4718608 | tf_op jit(solution)/shard_map/all_gather | solution.py:254
  523.9 17.1 pmax.7
  543.6 17.2 psum.57
  571.8 78.0 %reduce-scatter.4.cloned.1.call-done = bf16[768,768]{1,0:T(8,128)(2,1)} async-done(((bf16[3072,768]{1,0:T(8,128)(2,1)}), bf16[768,768]{1,0:T(8,128)(2,1)}) %reduce-scatter.4.cloned.1.call-update) | async-done | bytes 1179664 | tf_op jit(solution)/shard_map/reduce_scatter | solution.py:281
  661.5 12.7 add_convert_fusion.1
  700.5 11.3 multiply_convert_fusion.1
  754.1 11.9 add_convert_fusion
  792.2 11.2 multiply_convert_fusion
  868.9 12.0 concatenate.22
  880.9 10.1 bitcast_dynamic-update-slice_fusion.1
  910.7 10.3 bitcast_dynamic-update-slice_fusion
  930.3 23.5 %gather_fusion.5 = bf16[32,768,768]{1,2,0:T(8,128)(2,1)} fusion(bf16[24,768,768]{1,2,0:T(8,128)(2,1)} %convolution_dynamic-update-slice_fusion, s32[1024]{0:T(1024)} %get-tuple-element.187), kind=kCustom, calls=%fused_computation.5 | custom fusion | bytes 75497600 | tf_op jit(solution)/shard_map/jit(_take)/gather | solution.py:350
  958.8 25.5 %select_convert_fusion = bf16[32,768,768]{1,2,0:T(8,128)(2,1)} fusion(bf16[32,768,768]{1,2,0:T(8,128)(2,1)} %gather_fusion.5, pred[32]{0:T(512)(128)(4,1)S(1)} %copy-done.159, pred[32]{0:T(512)(128)(4,1)S(1)} %copy-done.158), kind=kLoop, calls=%fused_computation.6 | loop fusion | flops 37748736 | bytes 75497536 | tf_op jit(solution)/shard_map/convert_element_type | solution.py:350
  988.2 9.6 copy.187
  998.0 9.7 copy.185
  1010.7 9.6 copy.162
  1020.4 42.0 %all-reduce.1 = (f32[]{:T(128)}, f32[10,768]{1,0:T(8,128)S(1)}, f32[1024]{0:T(1024)S(1)}) all-reduce(f32[]{:T(128)} %multiply_reduce_fusion.17, f32[10,768]{1,0:T(8,128)S(1)} %concatenate.23, f32[1024]{0:T(1024)S(1)} %multiply_subtract_fusion.5), channel_id=1, replica_groups=mesh['dp'=8,'vocab'=4] {'dp','vocab'}, use_global_device_ids=true, to_apply=%region_23.24 | all-reduce | flops 8705 | bytes 69640 | tf_op jit(solution)/shard_map/psum | solution.py:346
  1063.7 10.9 multiply_subtract_fusion
  1074.7 34.4 %all-reduce.6.cloned.1.call-done = f32[256,768]{1,0:T(8,128)} async-done(((f32[256,768]{1,0:T(8,128)}), f32[256,768]{1,0:T(8,128)}) %all-reduce.6.cloned.1.call-update) | async-done | bytes 786448 | tf_op jit(solution)/shard_map/psum | solution.py:341
  1111.9 225.8 %reduce-scatter.6.cloned.1.call-done = bf16[4,768,768]{1,2,0:T(8,128)(2,1)} async-done(((bf16[32,768,768]{1,2,0:T(8,128)(2,1)}), bf16[4,768,768]{1,2,0:T(8,128)(2,1)}) %reduce-scatter.6.cloned.1.call-update) | async-done | bytes 4718608 | tf_op jit(solution)/shard_map/reduce_scatter | solution.py:349
  1337.7 321.6 %all-reduce.9 = f32[4,768,768]{1,2,0:T(8,128)} all-reduce(bf16[4,768,768]{1,2,0:T(8,128)(2,1)} %reduce-scatter.6.cloned.1.call-done), channel_id=1, replica_groups=mesh['dp'=8,'vocab'=4] {'vocab'}, use_global_device_ids=true, to_apply=%region_38.39 | all-reduce | flops 2359296 | bytes 14155776 | tf_op jit(solution)/shard_map/psum | solution.py:357
  1659.3 25.0 %broadcast_select_fusion.1 = (f32[4,768,768]{1,2,0:T(8,128)}, f32[4,768,768]{1,2,0:T(8,128)}, f32[4,768,768]{1,2,0:T(8,128)}) fusion(pred[4]{0:T(512)(128)(4,1)S(1)} %dynamic_slice.11, f32[4,768,768]{1,2,0:T(8,128)} %all-reduce.9, f32[4,768,768]{1,2,0:T(8,128)} %copy.185, f32[4,768,768]{1,2,0:T(8,128)} %copy.187, f32[]{:T(128)} %bitcast.38, f32[]{:T(128)} %bitcast.37, ...), kind=kLoop, calls=%fused_computation.83 | loop fusion | flops 42467328 | bytes 66060300 | tf_op jit(solution)/shard_map/jit(_where)/select_n | solution.py:373
  1684.3 9.6 copy.189
  1693.9 9.6 copy.190
  (553 shorter events, 392.6 us)
Async XLA Ops:
  7.2 42.8 %all-gather.5.cloned.1.call-start = ((), (), s32[]{:S(2)}) async-start(), calls=%async_computation.3 | async-start | bytes 1966080 | tf_op jit(solution)/shard_map/all_gather | solution.py:220
  9.2 221.8 %all-gather.7.cloned.1.call-start = ((), (), s32[]{:S(2)}) async-start(), calls=%async_computation.4 | async-start | bytes 42467328 | tf_op jit(solution)/shard_map/all_gather | solution.py:217
  15.6 503.9 %all-gather.9.cloned.1.call-start = ((), (), s32[]{:S(2)}) async-start(), calls=%async_computation.5 | async-start | bytes 5898240 | tf_op jit(solution)/shard_map/all_gather | solution.py:254
  21.2 43.5 %copy-start.83 = (s32[1024]{0:T(1024)}, s32[1024]{0:T(1024)S(1)}, u32[]{:S(2)}) copy-start(s32[1024]{0:T(1024)S(1)} %pad_clamp_fusion.1) | copy-start | bytes 12292
  22.7 247.0 %copy-start.115 = (f32[768]{0:T(1024)}, f32[768]{0:T(1024)S(1)}, u32[]{:S(2)}) copy-start(f32[768]{0:T(1024)S(1)} %get-tuple-element.106) | copy-start | bytes 9220
  22.7 247.0 %copy-start.144 = (f32[768]{0:T(1024)}, f32[768]{0:T(1024)S(1)}, u32[]{:S(2)}) copy-start(f32[768]{0:T(1024)S(1)} %get-tuple-element.105) | copy-start | bytes 9220
  22.7 282.0 %copy-start.113 = (f32[768]{0:T(1024)}, f32[768]{0:T(1024)S(1)}, u32[]{:S(2)}) copy-start(f32[768]{0:T(1024)S(1)} %get-tuple-element.104) | copy-start | bytes 9220
  22.7 282.0 %copy-start.142 = (f32[768]{0:T(1024)}, f32[768]{0:T(1024)S(1)}, u32[]{:S(2)}) copy-start(f32[768]{0:T(1024)S(1)} %get-tuple-element.103) | copy-start | bytes 9220
  22.7 323.6 %copy-start.111 = (f32[768]{0:T(1024)}, f32[768]{0:T(1024)S(1)}, u32[]{:S(2)}) copy-start(f32[768]{0:T(1024)S(1)} %get-tuple-element.102) | copy-start | bytes 9220
  22.7 323.6 %copy-start.140 = (f32[768]{0:T(1024)}, f32[768]{0:T(1024)S(1)}, u32[]{:S(2)}) copy-start(f32[768]{0:T(1024)S(1)} %get-tuple-element.101) | copy-start | bytes 9220
  22.8 358.6 %copy-start.108 = (f32[768]{0:T(1024)}, f32[768]{0:T(1024)S(1)}, u32[]{:S(2)}) copy-start(f32[768]{0:T(1024)S(1)} %get-tuple-element.100) | copy-start | bytes 9220
  22.8 358.6 %copy-start.138 = (f32[768]{0:T(1024)}, f32[768]{0:T(1024)S(1)}, u32[]{:S(2)}) copy-start(f32[768]{0:T(1024)S(1)} %get-tuple-element.99) | copy-start | bytes 9220
  62.1 207.7 %copy-start.122 = (f32[771]{0:T(1024)}, f32[771]{0:T(1024)S(1)}, u32[]{:S(2)}) copy-start(f32[771]{0:T(1024)S(1)} %div.188) | copy-start | bytes 9256
  64.8 205.0 %copy-start.124 = (f32[771]{0:T(1024)}, f32[771]{0:T(1024)S(1)}, u32[]{:S(2)}) copy-start(f32[771]{0:T(1024)S(1)} %rsqrt.55) | copy-start | bytes 9256
  423.7 95.9 %copy-start.51 = (bf16[256,768]{1,0:T(8,128)(2,1)S(1)}, bf16[256,768]{1,0:T(8,128)(2,1)}, u32[]{:S(2)}) copy-start(bf16[256,768]{1,0:T(8,128)(2,1)} %convert_element_type.194) | copy-start | bytes 1179652
  428.8 220.9 %reduce-scatter.4.cloned.1.call-start = ((), (), s32[]{:S(2)}) async-start(), calls=%async_computation.6 | async-start | bytes 5898240 | tf_op jit(solution)/shard_map/reduce_scatter | solution.py:281
  490.3 71.2 %copy-start.64 = (f32[4,1,768]{2,1,0:T(1,128)}, f32[4,1,768]{2,1,0:T(1,128)S(1)}, u32[]{:S(2)}) copy-start(f32[4,1,768]{2,1,0:T(1,128)S(1)} %convert_multiply_fusion) | copy-start | bytes 36868
  523.9 42.0 %copy-start.4 = (f32[3072,256]{0,1:T(8,128)}, f32[3072,256]{0,1:T(8,128)S(1)}, u32[]{:S(2)}) copy-start(f32[3072,256]{0,1:T(8,128)S(1)} %get-tuple-element.178) | copy-start | bytes 9437188
  566.0 387.9 %reduce-scatter.8.cloned.1.call-start = ((), (), s32[]{:S(2)}) async-start(), calls=%async_computation.8 | async-start | bytes 1966080 | tf_op jit(solution)/shard_map/reduce_scatter | solution.py:336
  566.6 83.1 %copy-start.102 = (f32[768]{0:T(1024)}, f32[768]{0:T(1024)S(1)}, u32[]{:S(2)}) copy-start(f32[768]{0:T(1024)S(1)} %mul.728) | copy-start | bytes 9220
  568.5 81.3 %copy-start.20 = (bf16[768,768]{1,0:T(8,128)(2,1)S(1)}, bf16[768,768]{1,0:T(8,128)(2,1)}, u32[]{:S(2)}) copy-start(bf16[768,768]{1,0:T(8,128)(2,1)} %gather_fusion.3) | copy-start | bytes 3538948
  861.0 202.7 %all-reduce.8.cloned.1.call-start = ((), (), s32[]{:S(2)}) async-start(), calls=%async_computation.10 | async-start | bytes 7766016 | tf_op jit(solution)/shard_map/psum | solution.py:346
  909.0 200.0 %all-reduce.6.cloned.1.call-start = ((), (), s32[]{:S(2)}) async-start(), calls=%async_computation.9 | async-start | bytes 1572864 | tf_op jit(solution)/shard_map/psum | solution.py:341
  958.8 378.9 %reduce-scatter.6.cloned.1.call-start = ((), (), s32[]{:S(2)}) async-start(), calls=%async_computation.7 | async-start | bytes 42467328 | tf_op jit(solution)/shard_map/reduce_scatter | solution.py:349
  1010.7 51.7 %copy-start.152 = (f32[1024]{0:T(1024)S(1)}, f32[1024]{0:T(1024)}, u32[]{:S(2)}) copy-start(f32[1024]{0:T(1024)} %param.41) | copy-start | bytes 12292
  1010.7 51.7 %copy-start.153 = (f32[1024]{0:T(1024)S(1)}, f32[1024]{0:T(1024)}, u32[]{:S(2)}) copy-start(f32[1024]{0:T(1024)} %param.40) | copy-start | bytes 12292
  1010.7 52.3 %copy-start.71 = (f32[10,768]{1,0:T(8,128)S(1)}, f32[10,768]{1,0:T(8,128)}, u32[]{:S(2)}) copy-start(f32[10,768]{1,0:T(8,128)} %param.36) | copy-start | bytes 92164
  1010.7 52.3 %copy-start.81 = (f32[10,768]{1,0:T(8,128)S(1)}, f32[10,768]{1,0:T(8,128)}, u32[]{:S(2)}) copy-start(f32[10,768]{1,0:T(8,128)} %param.38) | copy-start | bytes 92164
  1010.7 52.3 %copy-start.82 = (f32[10,768]{1,0:T(8,128)S(1)}, f32[10,768]{1,0:T(8,128)}, u32[]{:S(2)}) copy-start(f32[10,768]{1,0:T(8,128)} %param.37) | copy-start | bytes 92164
  1063.7 45.3 %copy-start.52 = (f32[256,768]{1,0:T(8,128)S(1)}, f32[256,768]{1,0:T(8,128)}, u32[]{:S(2)}) copy-start(f32[256,768]{1,0:T(8,128)} %param.30) | copy-start | bytes 2359300
  1063.7 45.3 %copy-start.54 = (f32[256,768]{1,0:T(8,128)S(1)}, f32[256,768]{1,0:T(8,128)}, u32[]{:S(2)}) copy-start(f32[256,768]{1,0:T(8,128)} %param.32) | copy-start | bytes 2359300
  1063.7 45.3 %copy-start.55 = (f32[256,768]{1,0:T(8,128)S(1)}, f32[256,768]{1,0:T(8,128)}, u32[]{:S(2)}) copy-start(f32[256,768]{1,0:T(8,128)} %param.31) | copy-start | bytes 2359300
  (147 other events, 1139.1 us)
Sparse Core Ops, SparseCore 0:
  10.2 39.7 all-gather.4
  52.5 178.4 all-gather.6
  428.9 90.5 all-gather.8
  566.1 83.5 reduce-scatter.3
  861.1 35.8 reduce-scatter.7
  909.2 141.0 all-reduce.7
  1054.2 54.7 all-reduce.5
  1113.1 224.5 reduce-scatter.5
where the time goes:
time: 1740 us; the launch traced here: 1720 us
  waiting for transfers between devices  557 us (32%)
  blocking collectives  455 us (26%)
  matrix products  245 us (14%)
  local copies, waits for them, and re-layouts  240 us (14%)
  other arithmetic  204 us (12%)
  between operations  18 us (1%)
    psum x1, blocking collectives, on_device(): owned = lax.psum(owned, 'vocab')  322 us
    reduce_scatter x1, waiting for transfers between devices, on_device(): lax.psum_scatter(jnp.where(filled[:, None, None], jnp.take(all_grads, blo...  226 us
    all_gather x1, waiting for transfers between devices, on_device(): lax.all_gather(master_block_weight.astype(jnp.bfloat16), 'dp', axis=0, ti...  163 us
    unnamed x352, local copies, waits for them, and re-layouts  84 us
    reduce_scatter x1, waiting for transfers between devices, on_device(): lax.psum_scatter(jnp.dot(grad_logits, local_table, preferred_element_type...  78 us
    convert_element_type x2, other arithmetic, layer_forward(): hidden = exact_gelu(up_proj).astype(jnp.bfloat16)  45.5 us
    psum x1, blocking collectives, on_device(): masked_total = lax.psum(jnp.sum(mask_float), ('dp', 'vocab'))  43.4 us
    psum x1, blocking collectives, on_device(): lax.psum((loss_part, extra_grad, norm_grad, bias_grad), ('dp', 'vocab'))  42 us
  transfers between devices with their start and end apart: 8, of which 6 were waited for; matrix products, arithmetic and copies ran while one was open for 12% of the time, Pallas kernels for 0%

commit v1 on v0

--- a/solution.py
+++ b/solution.py
@@ -1,8 +1,11 @@
+import functools
 import math
 
 import jax
 import jax.numpy as jnp
 from jax import lax
+from jax.experimental import pallas as pl
+from jax.experimental.pallas import tpu as pltpu
 from jax.sharding import PartitionSpec as P
 
 MODEL_WIDTH = 768
@@ -21,6 +24,742 @@
 BETA_TWO = 0.96
 ADAM_EPS = 1e-08
 DECAY = 0.045
+
+
+MESH = pl.DeviceIdType.MESH
+W = 768
+HALF = 384
+BF = jnp.bfloat16
+F32 = jnp.float32
+
+def place():
+    d = lax.axis_index("dp")
+    k = lax.axis_index("vocab")
+    q = d % 2
+    x = (d // 2) % 2
+    y = d // 4
+    chip_x = y * 2 + (1 - x)
+    chip_y = (1 - y) * 2 + x
+    chip_d = (1 - y) * 2 + (1 - x)
+    return d, k, q, d // 2, chip_x, chip_y, chip_d
+
+def barrier(d, k):
+    sem = pltpu.get_barrier_semaphore()
+    for i in range(1, 8):
+        pl.semaphore_signal(sem, inc=1, device_id=((d + i) % 8, k), device_id_type=MESH)
+    for i in range(1, 4):
+        pl.semaphore_signal(sem, inc=1, device_id=(d, (k + i) % 4), device_id_type=MESH)
+    pl.semaphore_wait(sem, 10)
+
+def remote(src, dst, s, r, dd, kk):
+    return pltpu.make_async_remote_copy(src_ref=src, dst_ref=dst, send_sem=s, recv_sem=r, device_id=(dd, kk), device_id_type=MESH)
+
+def rows(lo, n):
+    return pl.ds(pl.multiple_of(lo, 16), n)
+
+def half(q):
+    return pl.ds(pl.multiple_of(q * HALF, HALF), HALF)
+
+SEQ = 272
+REAL = 257
+ROWS = 3 * SEQ
+SCALE = HEAD_DIM ** (-0.5)
+WINDOW = ((0, 1), (0, 2), (1, 3), (2, 3), (3, 4), (3, 5), (4, 6), (5, 6))
+
+def dot(a, b):
+    return jnp.dot(a, b, preferred_element_type=F32)
+
+def dot_tb(a, b):
+    return lax.dot_general(a, b, (((1,), (1,)), ((), ())), preferred_element_type=F32)
+
+def dot_ta(a, b):
+    return lax.dot_general(a, b, (((0,), (0,)), ((), ())), preferred_element_type=F32)
+
+def loop(n, fn):
+    lax.fori_loop(0, n, lambda i, _: (fn(i), 0)[1], 0)
+
+def row_chunk(i):
+    return pl.ds(pl.multiple_of(i * 48, 16), 48)
+
+def normed(x):
+    centred = x - jnp.mean(x, -1, keepdims=True)
+    rstd = lax.rsqrt(jnp.mean(centred * centred, -1, keepdims=True) + NORM_EPS)
+    return centred * rstd, rstd
+
+def norm_into(out, x, norm_ref, row):
+    def one(i):
+        r = row_chunk(i)
+        out[r] = (normed(x[r])[0] * norm_ref[row:row + 1] + norm_ref[row + 1:row + 2]).astype(BF)
+    loop(ROWS // 48, one)
+
+def gelu_terms(u):
+    cdf = 0.5 * (1.0 + lax.erf(u * 2.0 ** -0.5))
+    return u * cdf, cdf + u * jnp.exp(-0.5 * u * u) * (2.0 * math.pi) ** -0.5
+
+def head_mask(h):
+    lo, hi = WINDOW[h]
+    lane = lax.broadcasted_iota(jnp.int32, (SEQ, (hi - lo) * 128), 1) + lo * 128
+    return (lane >= HEAD_DIM * h) & (lane < HEAD_DIM * (h + 1)), slice(lo * 128, hi * 128)
+
+def join_heads(ref, r, base, o, scale=1.0):
+    ref[r, base:base + 128] = ((o[0] + o[1][:, :128]) * scale).astype(BF)
+    ref[r, base + 128:base + 256] = ((o[1][:, 128:] + o[2][:, :128]) * scale).astype(BF)
+    ref[r, base + 256:base + 384] = ((o[2][:, 128:] + o[3]) * scale).astype(BF)
+
+def attend(i, q, k, v, att, probs):
+    r = pl.ds(pl.multiple_of(i * SEQ, 16), SEQ)
+    real = lax.broadcasted_iota(jnp.int32, (SEQ, SEQ), 1) < REAL
+    zero = jnp.zeros((), BF)
+    for base in range(2):
+        outs = []
+        for h in range(4 * base, 4 * base + 4):
+            m, cs = head_mask(h)
+            s = jnp.where(real, dot_tb(jnp.where(m, q[r, cs], zero), k[r, cs]), -1e30)
+            e = jnp.exp((s - jnp.max(s, axis=1, keepdims=True)) * SCALE)
+            p = (e * (1.0 / jnp.sum(e, axis=1, keepdims=True))).astype(BF)
+            probs[i, h] = p
+            outs.append(dot(p, jnp.where(m, v[r, cs], zero)))
+        join_heads(att, r, 384 * base, outs)
+
+def attend_back(base, i, q, k, v, probs, do, dq, dk, dv):
+    r = pl.ds(pl.multiple_of(i * SEQ, 16), SEQ)
+    zero = jnp.zeros((), BF)
+    oq, ok, ov = [], [], []
+    for h in range(4 * base, 4 * base + 4):
+        m, cs = head_mask(h)
+        p = probs[i, h]
+        dom = jnp.where(m, do[r, cs], zero)
+        pf = p.astype(F32)
+        w = pf * dot_tb(dom, v[r, cs])
+        ds = (w - pf * jnp.sum(w, axis=1, keepdims=True)).astype(BF)
+        oq.append(dot(ds, jnp.where(m, k[r, cs], zero)))
+        ok.append(dot_ta(ds, jnp.where(m, q[r, cs], zero)))
+        ov.append(dot_ta(p, dom))
+    join_heads(dq, r, 384 * base, oq, SCALE)
+    join_heads(dk, r, 384 * base, ok, SCALE)
+    join_heads(dv, r, 384 * base, ov)
+
+class Moves:
+    def __init__(self, sems):
+        self.sems, self.index, self.busy = sems, {}, {}
+    def start(self, name, src, dst):
+        self.free(name)
+        i = self.index.setdefault(name, len(self.index))
+        self.busy[name] = pltpu.make_async_copy(src, dst, self.sems.at[i])
+        self.busy[name].start()
+    def free(self, *names):
+        for n in names or list(self.busy):
+            if n in self.busy:
+                self.busy.pop(n).wait()
+
+class Weights:
+    def __init__(self, moves, wall, ring, order, ready=lambda b: None):
+        self.moves, self.wall, self.ring, self.order, self.ready = moves, wall, ring, order, ready
+        self.slots, self.next, self.used = ring.shape[0], 0, 0
+    def fill(self, ahead):
+        while self.next < min(len(self.order), self.used + ahead):
+            b = self.order[self.next]
+            self.ready(b)
+            s = self.next % self.slots
+            self.moves.start(("w", s), self.wall.at[b], self.ring.at[s])
+            self.next += 1
+    def take(self, b):
+        assert self.order[self.used] == b
+        self.fill(1)
+        s = self.used % self.slots
+        self.moves.free(("w", s))
+        self.used += 1
+        self.fill(self.slots - 1)
+        return self.ring.at[s]
+
+def is_late(b):
+    return b >= 6 and b % 2 == 1
+
+class Gatherer:
+    def __init__(self, at, wall, chunk, sems):
+        self.d, self.k, self.q, self.c, self.cx, self.cy, self.cd = at
+        self.wall, self.chunk, self.sems = wall, chunk, sems
+        self.kp = self.k % 2
+        self.peer = self.k + 1 - 2 * self.kp
+        self.xn, self.yn, self.partner = self.cx * 2 + self.q, self.cy * 2 + self.q, self.c * 2 + (1 - self.q)
+        self.cols = half(self.q)
+        self.sent, self.own = {}, []
+        self.nxy = self.nfw = self.nco = self.nzl = 0
+    def send(self, stage, b, j, src, dst, dd, kk):
+        i = b * 8 + stage + j
+        cp = remote(src, dst, self.sems.at[0, i], self.sems.at[1, i], dd, kk)
+        cp.start()
+        self.sent.setdefault((b, stage), []).append(cp)
+    def arrived(self, b, stage):
+        for cp in self.sent[b, stage]:
+            cp.wait_recv()
+    def move(self, stage, b, j, reg, dd):
+        self.send(stage, b, j, reg, reg, dd, self.k)
+    def begin(self, own_sems):
+        for b in range(24):
+            dst = self.wall.at[b, self.c, self.kp, :, self.cols]
+            o = pltpu.make_async_copy(self.chunk.at[b], dst, own_sems.at[b])
+            o.start()
+            self.own.append(o)
+            if not is_late(b):
+                self.send(0, b, 0, self.chunk.at[b], dst, self.d, self.peer)
+    def xy(self, b):
+        self.own[b].wait()
+        if is_late(b):
+            reg = self.wall.at[b, self.c, self.kp, :, self.cols]
+        else:
+            self.arrived(b, 0)
+            reg = self.wall.at[b, self.c, :, :, self.cols]
+        self.move(1, b, 0, reg, self.xn)
+        self.move(1, b, 1, reg, self.yn)
+    def fw(self, b):
+        self.arrived(b, 1)
+        if is_late(b):
+            self.move(3, b, 0, self.wall.at[b, self.cx, self.kp, pl.ds(0, 48), self.cols], self.yn)
+            self.move(3, b, 1, self.wall.at[b, self.cy, self.kp, pl.ds(48, 48), self.cols], self.xn)
+        else:
+            self.move(3, b, 0, self.wall.at[b, self.cx, 0, :, self.cols], self.yn)
+            self.move(3, b, 1, self.wall.at[b, self.cy, 1, :, self.cols], self.xn)
+    def zl(self, b):
+        if is_late(b):
+            self.arrived(b, 3)
+            reg = self.wall.at[b, :, self.kp, :, self.cols]
+            self.send(5, b, 0, reg, reg, self.d, self.peer)
+    def co(self, b):
+        self.arrived(b, 5 if is_late(b) else 3)
+        self.move(6, b, 0, self.wall.at[b, :, :, :, self.cols], self.partner)
+    def advance(self, nxy, nfw, nzl, nco):
+        while self.nxy < min(nxy, 24):
+            self.xy(self.nxy)
+            self.nxy += 1
+        while self.nfw < min(nfw, 24):
+            self.fw(self.nfw)
+            self.nfw += 1
+        while self.nzl < min(nzl, 24):
+            self.zl(self.nzl)
+            self.nzl += 1
+        while self.nco < min(nco, 24):
+            self.co(self.nco)
+            self.nco += 1
+    def finish(self):
+        for cps in self.sent.values():
+            for cp in cps:
+                cp.wait_send()
+
+AHEAD = ((2, 1, 1, 0), (8, 5, 3, 1))
+
+def forward_kernel(slot_ref, send_ref, table_ref, count_ref, ids_ref, mask_ref, pos_ref, few_ref, norm_ref,
+                   wall, full_ref, total_ref, stream0, stream1, stream2, middles, lns, qkvs, atts, probs_out, hids, slopes,
+                   st, mid, up, ln, qkv, att, probs, hid, slope, ring, sems, slots, chunk, cnt, own_sems, g_sems,
+                   a2a_s, a2a_r, t_s, t_r, tp_s, tp_r, tc_s, tc_r, n_s, n_r, np_s, np_r):
+    at = place()
+    d, k, q, c, cx, cy, cd = at
+    ga = Gatherer(at, wall, chunk, g_sems)
+    cols = ga.cols
+    xn, yn, dn, partner = ga.xn, ga.yn, cd * 2 + q, ga.partner
+    barrier(d, k)
+    mv = Moves(sems)
+    started = []
+    def go(cp):
+        cp.start()
+        started.append(cp)
+        return cp
+    trow = rows(k * 256 + c * 64, 64)
+    tz = [go(remote(table_ref.at[rows(c * 64, 64), cols], full_ref.at[trow, cols], t_s.at[i], t_r.at[i], d, (k + i) % 4)) for i in range(1, 4)]
+    nz = [go(remote(count_ref, cnt.at[k, d], n_s.at[i], n_r.at[i], d, (k + i) % 4)) for i in range(1, 4)]
+    a2a = []
+    for i in range(1, 8):
+        t = (d + i) % 8
+        a2a.append(go(remote(send_ref.at[:, t // 2, :, half(t % 2)], slots.at[d], a2a_s.at[i], a2a_r.at[i], t, k)))
+    mv.start("mine", send_ref.at[:, c, :, cols], slots.at[d])
+    mv.start("tmine", table_ref, full_ref.at[rows(k * 256, 256)])
+    cnt[k, d] = count_ref[...]
+    for cp in tz:
+        cp.wait_recv()
+    tps = []
+    for i in range(1, 4):
+        rr = full_ref.at[rows(((k + i) % 4) * 256 + c * 64, 64), cols]
+        for j, t in enumerate((xn, yn, dn)):
+            tps.append(go(remote(rr, rr, tp_s.at[i, j], tp_r.at[i, j], t, k)))
+    for cp in nz:
+        cp.wait_recv()
+    npl = [go(remote(cnt.at[:, d], cnt.at[:, d], np_s.at[i], np_r.at[i], (d + i) % 8, k)) for i in range(1, 8)]
+    for i in range(3):
+        def base(j, i=i):
+            r, p = pl.ds(pl.multiple_of(SEQ * i + j * 16, 16), 16), pl.ds(pl.multiple_of(j * 16, 16), 16)
+            st[r] = pos_ref[p] + mask_ref[r] * few_ref[3:4]
+        loop(17, base)
+        st[SEQ * i + 256:SEQ * i + 257] = pos_ref[256:257] + few_ref[i:i + 1]
+    mv.free("mine")
+    for cp in a2a:
+        cp.wait_recv()
+    for b in range(24):
+        s = slot_ref[b]
+        chunk[b] = slots[s // 4, s % 4]
+    ga.begin(own_sems)
+    mv.free("tmine")
+    for cp in tps:
+        cp.wait_recv()
+    tcs = []
+    for i in range(1, 4):
+        rr = full_ref.at[rows(((k + i) % 4) * 256, 256), cols]
+        tcs.append(go(remote(rr, rr, tc_s.at[i], tc_r.at[i], partner, k)))
+    ga.advance(3, 0, 0, 0)
+    for cp in npl:
+        cp.wait_recv()
+    total_ref[...] = jnp.sum(cnt[...], axis=(0, 1))
+    for cp in tcs:
+        cp.wait_recv()
+    hot = (lax.broadcasted_iota(jnp.int32, (ROWS, CODES), 1) == ids_ref[...]).astype(BF)
+    for n in range(3):
+        cs = slice(256 * n, 256 * n + 256)
+        st[:, cs] = st[:, cs] + math.sqrt(MODEL_WIDTH) * dot(hot, full_ref[:, cs])
+    mv.start("st", st, stream0)
+    nslots = ring.shape[0]
+    def step(t):
+        lo, hi = AHEAD
+        n = [min(a + t, b) for a, b in zip(lo, hi)]
+        ga.advance(*(t + 1 + x for x in n))
+    def fetch(b):
+        if b < 24:
+            step(b)
+            ga.arrived(b, 6)
+            mv.start(("w", b % nslots), wall.at[b], ring.at[b % nslots])
+    def weight(b, n):
+        if n == 0:
+            mv.free(("w", b % nslots))
+        if n == 1:
+            fetch(b + 1)
+        return ring[b % nslots, :, :, :, 256 * n:256 * n + 256].reshape(W, 256)
+    ga.advance(3, 1, 0, 0)
+    for l in range(LAYERS):
+        base = 12 * l
+        mv.free("st")
+        if l:
+            mv.start("st", st, stream1)
+        mv.free("ln0")
+        norm_into(ln.at[0], st, norm_ref, 4 * l)
+        mv.start("ln0", ln.at[0], lns.at[l, 0])
+        if l == 0:
+            fetch(0)
+        for j in range(3):
+            mv.free(("qkv", j))
+            for n in range(3):
+                cs = slice(256 * n, 256 * n + 256)
+                qkv[j, :, cs] = dot(ln[0], weight(base + j, n)).astype(BF)
+            mv.start(("qkv", j), qkv.at[j], qkvs.at[l, j])
+        mv.free("att", "probs")
+        loop(3, lambda i: attend(i, qkv.at[0], qkv.at[1], qkv.at[2], att, probs))
+        mv.start("att", att, atts.at[l])
+        mv.start("probs", probs, probs_out.at[l])
+        mv.free("mid")
+        for n in range(3):
+            cs = slice(256 * n, 256 * n + 256)
+            mid[:, cs] = st[:, cs] + dot(att[...], weight(base + 3, n))
+        mv.start("mid", mid, middles.at[l])
+        mv.free("ln1")
+        norm_into(ln.at[1], mid, norm_ref, 4 * l + 2)
+        mv.start("ln1", ln.at[1], lns.at[l, 1])
+        for j in range(4):
+            for n in range(3):
+                cs = slice(256 * n, 256 * n + 256)
+                up[:, cs] = dot(ln[1], weight(base + 4 + j, n))
+            mv.free(("hid", j), ("slope", j))
+            def gelu(i, j=j):
+                r = row_chunk(i)
+                h, g = gelu_terms(up[r])
+                hid[j, r] = h.astype(BF)
+                slope[j, r] = g.astype(BF)
+            loop(ROWS // 48, gelu)
+            mv.start(("hid", j), hid.at[j], hids.at[l, j])
+            mv.start(("slope", j), slope.at[j], slopes.at[l, j])
+        mv.free("st")
+        for j in range(4):
+            for n in range(3):
+                cs = slice(256 * n, 256 * n + 256)
+                st[:, cs] = (st if j else mid)[:, cs] + dot(hid[j], weight(base + 8 + j, n))
+    mv.start("st", st, stream2)
+    ga.finish()
+    for cp in started:
+        cp.wait_send()
+    mv.free()
+
+def forward(slot_of, send, table, count, ids, mask, pos, few, norms):
+    S = jax.ShapeDtypeStruct
+    V = pltpu.VMEM
+    D = pltpu.SemaphoreType.DMA
+    any_ = pl.BlockSpec(memory_space=pl.ANY)
+    vm = pl.BlockSpec(memory_space=pltpu.VMEM)
+    shapes = (S((24, 4, 2, 96, W), BF), S((CODES, W), BF), S((8, 128), F32), S((ROWS, W), F32),
+              S((ROWS, W), F32), S((ROWS, W), F32), S((2, ROWS, W), F32), S((2, 2, ROWS, W), BF), S((2, 3, ROWS, W), BF),
+              S((2, ROWS, W), BF), S((2, 3, 8, SEQ, SEQ), BF), S((2, 4, ROWS, W), BF), S((2, 4, ROWS, W), BF))
+    f32 = V((ROWS, W), F32)
+    return pl.pallas_call(
+        forward_kernel, out_shape=shapes,
+        in_specs=[pl.BlockSpec(memory_space=pltpu.SMEM), any_, any_] + [vm] * 6, out_specs=(any_, vm, vm) + (any_,) * 10,
+        scratch_shapes=[f32, f32, f32, V((2, ROWS, W), BF), V((3, ROWS, W), BF), V((ROWS, W), BF),
+                        V((3, 8, SEQ, SEQ), BF), V((4, ROWS, W), BF), V((4, ROWS, W), BF), V((3, 4, 2, 96, W), BF), D((32,)),
+                        V((8, 4, 96, HALF), BF), V((24, 96, HALF), BF), V((4, 8, 8, 128), F32), D((24,)), D((2, 192)),
+                        D((8,)), D((8,)), D((4,)), D((4,)), D((4, 3)), D((4, 3)), D((4,)), D((4,)), D((4,)), D((4,)), D((8,)), D((8,))],
+        compiler_params=pltpu.CompilerParams(collective_id=0, has_side_effects=True, vmem_limit_bytes=60 * 2**20),
+        cost_estimate=pl.CostEstimate(flops=24 * 2 * ROWS * W * W, bytes_accessed=100 * 10**6, transcendentals=10**7),
+        name="layers",
+    )(slot_of, send, table, count, ids, mask, pos, few, norms)
+
+def chunks_to_send(master):
+    part = master.reshape(4, 4, 2, 96, W)
+    return lax.dynamic_index_in_dim(part, lax.axis_index("vocab") % 2, 2, keepdims=False).astype(BF)
+
+def norm_back(x, dy, add, out, norm_ref, row, dnorm):
+    def one(i, carry):
+        r = row_chunk(i)
+        xhat, rstd = normed(x[r])
+        g = dy[r]
+        a = g * norm_ref[row:row + 1]
+        out[r] = add[r] + rstd * (a - jnp.mean(a, -1, keepdims=True) - xhat * jnp.mean(a * xhat, -1, keepdims=True))
+        return (carry[0] + jnp.sum((g * xhat).reshape(6, 8, W), 0), carry[1] + jnp.sum(g.reshape(6, 8, W), 0))
+    zero = jnp.zeros((8, W), F32)
+    gain, shift = lax.fori_loop(0, ROWS // 48, one, (zero, zero))
+    dnorm[row:row + 1] = jnp.sum(gain, 0, keepdims=True)
+    dnorm[row + 1:row + 2] = jnp.sum(shift, 0, keepdims=True)
+
+def round_into(out, x):
+    def one(i):
+        out[row_chunk(i)] = x[row_chunk(i)].astype(BF)
+    loop(ROWS // 48, one)
+
+LAGS = (1, 3, 5, 7, 9)
+
+class Reducer:
+    def __init__(self, mv, at, dring, sums, tmps, vv, land, sems):
+        self.mv, self.dring, self.sums, self.vv, self.sems = mv, dring, sums, vv, sems
+        self.d, self.k, self.q, self.c, self.cx, self.cy, self.cd = at
+        self.tc, self.td, self.te, self.tf = tmps
+        self.cb, self.dv, self.ev, self.f1, self.f2 = land
+        q = self.q
+        self.xn, self.yn, self.partner = self.cx * 2 + q, self.cy * 2 + q, self.c * 2 + (1 - q)
+        self.kp = self.k % 2
+        self.peer, self.cross = self.k + 1 - 2 * self.kp, (self.k + 2) % 4
+        self.mine, self.other = half(q), half(1 - q)
+        self.sent, self.blocks, self.born, self.n = {}, [], [], 0
+    def send(self, stage, u, j, src, dst, dd, kk):
+        i = u * 8 + stage + j
+        cp = remote(src, dst, self.sems.at[0, i], self.sems.at[1, i], dd, kk)
+        cp.start()
+        self.sent.setdefault((u, stage), []).append(cp)
+    def arrived(self, u, stage):
+        for cp in self.sent[u, stage]:
+            cp.wait_recv()
+    def gone(self, u, *stages):
+        for s in stages:
+            for cp in self.sent[u, s]:
+                cp.wait_send()
+    def slot(self):
+        n = len(self.blocks)
+        s = n % self.dring.shape[0]
+        if n >= self.dring.shape[0]:
+            self.gone(n - self.dring.shape[0], 0)
+        return self.dring.at[s]
+    def made(self, b):
+        u = len(self.blocks)
+        self.blocks.append(b)
+        self.born.append(self.n)
+        self.send(0, u, 0, self.dring.at[u % self.dring.shape[0], :, self.other], self.cb.at[b], self.partner, self.k)
+    def units(self):
+        return [(i, u) for i, lag in enumerate(LAGS) for u, t in enumerate(self.born) if t + lag == self.n]
+    def before(self):
+        for i, u in reversed(self.units()):
+            b = self.blocks[u]
+            self.arrived(u, (0, 1, 3, 5, 6)[i])
+            if i == 0:
+                self.mv.start("tc", self.cb.at[b], self.tc)
+            elif i == 1:
+                self.mv.start("td0", self.dv.at[0, b], self.td.at[0])
+                self.mv.start("td1", self.dv.at[1, b], self.td.at[1])
+            elif i == 2:
+                self.mv.start("te0", self.ev.at[0, b], self.te.at[0])
+                self.mv.start("te1", self.ev.at[1, b], self.te.at[1])
+            elif i == 3:
+                self.mv.start("tf0", self.f1.at[b], self.tf.at[0])
+            else:
+                self.mv.start("tf1", self.f2.at[b], self.tf.at[1])
+    def after(self):
+        c, cx, cy, cd, kp, k = self.c, self.cx, self.cy, self.cd, self.kp, self.k
+        ns = self.sums.shape[0]
+        for i, u in reversed(self.units()):
+            b, s = self.blocks[u], self.sums.at[u % ns]
+            if i == 0:
+                if u >= ns:
+                    self.gone(u - ns, 1, 3, 5, 6)
+                self.mv.free("tc")
+                own = self.dring.at[u % self.dring.shape[0]]
+                def one(j):
+                    r = rows(j * 96, 96)
+                    s[r] = own[r, self.mine] + self.tc[r]
+                loop(8, one)
+                self.send(1, u, 0, s.at[rows(192 * cd, 96)], self.dv.at[0, b], self.xn, k)
+                self.send(1, u, 1, s.at[rows(192 * cd + 96, 96)], self.dv.at[1, b], self.yn, k)
+            elif i == 1:
+                self.mv.free("td0", "td1")
+                r = rows(192 * cy, 96)
+                s[r] = s[r] + self.td[0]
+                r = rows(192 * cx + 96, 96)
+                s[r] = s[r] + self.td[1]
+                self.send(3, u, 0, s.at[rows(192 * cx, 192)], self.ev.at[0, b], self.xn, k)
+                self.send(3, u, 1, s.at[rows(192 * cy, 192)], self.ev.at[1, b], self.yn, k)
+            elif i == 2:
+                self.mv.free("te0", "te1")
+                def three(j):
+                    r, p = rows(192 * c + j * 96, 96), rows(j * 96, 96)
+                    s[r] = (s[r].astype(F32) + self.te[0, p].astype(F32) + self.te[1, p].astype(F32)).astype(BF)
+                loop(2, three)
+                self.send(5, u, 0, s.at[rows(192 * c + 96 * (1 - kp), 96)], self.f1.at[b], self.d, self.peer)
+            elif i == 3:
+                self.mv.free("tf0")
+                r = rows(192 * c + 96 * kp, 96)
+                s[r] = s[r] + self.tf[0]
+                self.send(6, u, 0, s.at[r], self.f2.at[b], self.d, self.cross)
+            else:
+                self.mv.free("tf1")
+                p = rows(96 * kp, 96)
+                self.vv[b, p] = s[rows(192 * c + 96 * kp, 96)] + self.tf[1]
+                self.send(7, u, 0, self.vv.at[b, p], self.vv.at[b, p], self.d, self.peer)
+        self.n += 1
+    def finish(self):
+        ns = self.sums.shape[0]
+        for u in range(24):
+            self.arrived(u, 7)
+            self.gone(u, 7)
+            if u >= 24 - self.dring.shape[0]:
+                self.gone(u, 0)
+            if u >= 24 - ns:
+                self.gone(u, 1, 3, 5, 6)
+
+def backward_kernel(block_ref, ids_ref, mask_ref, tail_ref, classes_ref, norm_ref, g_ref, head_ref, x0, x1, wall, middles, lns, qkvs, atts, probs_in, hids, slopes,
+                    own_ref, tout_ref, mout_ref, cout_ref, cb, dv, ev, f1, f2,
+                    g, acc, xs, low, ln, hid, slope, qkv, dqkv, att, probs, ring, dring, sums, tc, td, te, tf, vv,
+                    dnorm, tcb, tz, tp, mb, mc, me, mz, kb, sems, red_sems, o_s, o_r,
+                    t_s, t_r, tz_s, tz_r, tr_s, tr_r, tg_s, tg_r, m_s, m_r, mr_s, mr_r, mz_s, mz_r, mg_s, mg_r, k_s, k_r, kp_s, kp_r):
+    at = place()
+    d, k, q, c, cx, cy, cd = at
+    barrier(d, k)
+    mv = Moves(sems)
+    order = []
+    for l in reversed(range(LAYERS)):
+        for j in range(4):
+            order += [12 * l + 8 + j, 12 * l + 4 + j]
+        order += [12 * l + 3, 12 * l, 12 * l + 1, 12 * l + 2]
+    ws = Weights(mv, wall, ring, order)
+    red = Reducer(mv, at, dring, sums, (tc, td, te, tf), vv, (cb, dv, ev, f1, f2), red_sems)
+    xn, yn, dn, partner = red.xn, red.yn, cd * 2 + q, red.partner
+    mine, other = red.mine, red.other
+    started = []
+    def go(cp):
+        cp.start()
+        started.append(cp)
+        return cp
+    def weight_grad(b, a, cc):
+        out = red.slot()
+        red.before()
+        for n in range(3):
+            cs = slice(256 * n, 256 * n + 256)
+            out[:, cs] = dot_ta(a[...], cc[:, cs]).astype(BF)
+        red.made(b)
+        red.after()
+    def product(out, a, w, more):
+        for n in range(3):
+            cs = slice(256 * n, 256 * n + 256)
+            v = dot_tb(a[...], w[cs, :])
+            out[:, cs] = out[:, cs] + v if more else v
+    def chunk(l, j):
+        mv.start(("hid", j % 2), hids.at[l, j], hid.at[j % 2])
+        mv.start(("slope", j % 2), slopes.at[l, j], slope.at[j % 2])
+    gu = dqkv.at[0]
+    mv.start("g", g_ref, g)
+    chunk(1, 0)
+    ws.fill(3)
+    for l in reversed(range(LAYERS)):
+        base = 12 * l
+        mv.start("ln", lns.at[l, 1], ln)
+        mv.start("xs", middles.at[l], xs)
+        mv.start("att", atts.at[l], att)
+        mv.start("probs", probs_in.at[l], probs)
+        for j in range(3):
+            mv.start(("qkv", j), qkvs.at[l, j], qkv.at[j])
+        mv.free("g")
+        round_into(low, g)
+        mv.free("ln")
+        for j in range(4):
+            if j < 3:
+                chunk(l, j + 1)
+            elif l:
+                chunk(l - 1, 0)
+            mv.free(("hid", j % 2), ("slope", j % 2))
+            w = ws.take(base + 8 + j)
+            for n in range(3):
+                cs = slice(256 * n, 256 * n + 256)
+                gu[:, cs] = (dot_tb(low[...], w[cs, :]) * slope[j % 2, :, cs].astype(F32)).astype(BF)
+            weight_grad(base + 8 + j, hid.at[j % 2], low)
+            product(acc, gu, ws.take(base + 4 + j), j > 0)
+            weight_grad(base + 4 + j, ln, gu)
+        mv.start("ln", lns.at[l, 0], ln)
+        mv.free("xs")
+        norm_back(xs, acc, g, g, norm_ref, 4 * l + 2, dnorm)
+        mv.start("xs", (x1 if l else x0), xs)
+        round_into(low, g)
+        mv.free("att")
+        weight_grad(base + 3, att, low)
+        w = ws.take(base + 3)
+        for n in range(3):
+            cs = slice(256 * n, 256 * n + 256)
+            att[:, cs] = dot_tb(low[...], w[cs, :]).astype(BF)
+        mv.free("probs", ("qkv", 0), ("qkv", 1), ("qkv", 2))
+        for part in range(2):
+            red.before()
+            loop(3, lambda i: attend_back(part, i, qkv.at[0], qkv.at[1], qkv.at[2], probs, att, dqkv.at[0], dqkv.at[1], dqkv.at[2]))
+            red.after()
+        mv.free("ln")
+        for j in range(3):
+            product(acc, dqkv.at[j], ws.take(base + j), j > 0)
+            weight_grad(base + j, ln, dqkv.at[j])
+        mv.free("xs")
+        norm_back(xs, acc, g, g, norm_ref, 4 * l, dnorm)
+    mv.start("acc", head_ref.at[pl.ds(512, 512)], acc.at[pl.ds(0, 512)])
+    round_into(low, g)
+    for i in range(3):
+        row = g[SEQ * i + 256:SEQ * i + 257].astype(BF).astype(F32)
+        for t in range(6):
+            kb[6 * i + t:6 * i + t + 1] = row[:, 128 * t:128 * t + 128]
+    kb[18:24] = classes_ref[0:6]
+    cout_ref[k, d] = kb[...]
+    kz = [go(remote(kb, cout_ref.at[k, d], k_s.at[i], k_r.at[i], d, (k + i) % 4)) for i in range(1, 4)]
+    def position(i):
+        r = pl.ds(pl.multiple_of(i * 16, 16), 16)
+        xs[r] = g[r] + g[pl.ds(pl.multiple_of(i * 16 + SEQ, 16), 16)] + g[pl.ds(pl.multiple_of(i * 16 + 2 * SEQ, 16), 16)]
+    loop(17, position)
+    mb[1:257] = xs[0:256]
+    mb[0:1] = xs[256:257]
+    mb[257:258] = dot(mask_ref[...], low[...])[0:1]
+    mb[258:264] = jnp.zeros((6, W), F32)
+    mb[264:280] = tail_ref[...]
+    mb[265:273] = dnorm[0:8]
+    mb[280:288] = jnp.zeros((8, W), F32)
+    mcore = go(remote(mb.at[:, other], mc, m_s, m_r, partner, k))
+    mv.start("xs", head_ref.at[pl.ds(0, 512)], xs.at[pl.ds(0, 512)])
+    red.before()
+    red.after()
+    mv.free("xs", "acc")
+    tcore = []
+    for hf in range(2):
+        code = lax.broadcasted_iota(jnp.int32, (ROWS, 512), 1) + 512 * hf
+        hot = (code == ids_ref[...]).astype(BF)
+        part = (xs, acc)[hf]
+        buf = dqkv.at[hf]
+        for n in range(3):
+            cs = slice(256 * n, 256 * n + 256)
+            buf[0:512, cs] = (math.sqrt(MODEL_WIDTH) * dot_ta(hot, low[:, cs]) + part[0:512, cs]).astype(BF)
+        tcore.append(go(remote(buf.at[pl.ds(0, 512), other], tcb.at[pl.ds(512 * hf, 512)], t_s.at[hf], t_r.at[hf], partner, k)))
+    red.before()
+    red.after()
+    mcore.wait_recv()
+    for j in range(4):
+        r = pl.ds(j * 72, 72)
+        mc[r] = mc[r] + mb[r, mine]
+    mr = [go(remote(mc.at[pl.ds(pl.multiple_of(cc * 72, 8), 72)], me.at[j], mr_s.at[j], mr_r.at[j], t, k))
+          for j, (cc, t) in enumerate(((cx, xn), (cy, yn), (cd, dn)))]
+    for cp in tcore:
+        cp.wait_recv()
+    for hf in range(2):
+        def t_add(i, hf=hf):
+            r = rows(i * 64, 64)
+            s = rows(512 * hf + i * 64, 64)
+            tcb[s] = tcb[s] + dqkv[hf, r, mine]
+        loop(8, t_add)
+    tzs = [go(remote(tcb.at[rows(((k + i) % 4) * 256, 256)], tz.at[i - 1], tz_s.at[i], tz_r.at[i], d, (k + i) % 4)) for i in range(1, 4)]
+    red.before()
+    red.after()
+    for cp in kz:
+        cp.wait_recv()
+    kps = [go(remote(cout_ref.at[:, d], cout_ref.at[:, d], kp_s.at[i], kp_r.at[i], (d + i) % 8, k)) for i in range(1, 8)]
+    for cp in mr:
+        cp.wait_recv()
+    mz[k] = mc[pl.ds(pl.multiple_of(c * 72, 8), 72)] + me[0] + me[1] + me[2]
+    mzs = [go(remote(mz.at[k], mz.at[k], mz_s.at[i], mz_r.at[i], d, (k + i) % 4)) for i in range(1, 4)]
+    while red.n <= red.born[-1] + LAGS[-1]:
+        red.before()
+        red.after()
+    for cp in mzs:
+        cp.wait_recv()
+    r = pl.ds(pl.multiple_of(c * 72, 8), 72)
+    mout_ref[r, mine] = (mz[0] + mz[1]) + (mz[2] + mz[3])
+    reg = mout_ref.at[r, mine]
+    mgs = [go(remote(reg, reg, mg_s.at[j], mg_r.at[j], t, k)) for j, t in enumerate((xn, yn, dn))]
+    for cp in tzs:
+        cp.wait_recv()
+    def t_sum(i):
+        r = rows(i * 64, 64)
+        s = rows(256 * k + i * 64, 64)
+        tcb[s] = (tcb[s].astype(F32) + tz[0, r].astype(F32) + tz[1, r].astype(F32) + tz[2, r].astype(F32)).astype(BF)
+    loop(4, t_sum)
+    trs = [go(remote(tcb.at[rows(256 * k + 64 * cc, 64)], tp.at[j], tr_s.at[j], tr_r.at[j], t, k))
+           for j, (cc, t) in enumerate(((cx, xn), (cy, yn), (cd, dn)))]
+    red.finish()
+    outs = []
+    for i in (4, 5, 6, 7, 2, 3, 1, 0):
+        o = (d + i) % 8
+        s = i // 2
+        cols = slice(HALF * (i % 2), HALF * (i % 2) + HALF)
+        for j in range(4):
+            ring[s, 192 * j:192 * j + 192, cols] = vv[block_ref[o * 4 + j]]
+        for j in range(4):
+            src = ring.at[s, pl.ds(192 * j, 192), cols]
+            dst = own_ref.at[j, rows(192 * c, 192), mine]
+            if i:
+                outs.append(go(remote(src, dst, o_s.at[i, j], o_r.at[i, j], o, k)))
+            else:
+                mv.start(("own", j), src, dst)
+    for cp in trs:
+        cp.wait_recv()
+    tout_ref[rows(64 * c, 64), mine] = (tcb[rows(256 * k + 64 * c, 64)].astype(F32) + tp[0].astype(F32) + tp[1].astype(F32) + tp[2].astype(F32))
+    reg = tout_ref.at[rows(64 * c, 64), mine]
+    tgs = [go(remote(reg, reg, tg_s.at[j], tg_r.at[j], t, k)) for j, t in enumerate((xn, yn, dn))]
+    for cp in mgs + tgs:
+        cp.wait_recv()
+    reg = tout_ref.at[:, mine]
+    last = [go(remote(reg, reg, tg_s.at[3], tg_r.at[3], partner, k))]
+    reg = mout_ref.at[:, mine]
+    last.append(go(remote(reg, reg, mg_s.at[3], mg_r.at[3], partner, k)))
+    for cp in kps + outs + last:
+        cp.wait_recv()
+    for cp in started:
+        cp.wait_send()
+    mv.free()
+
+def backward(block_of, ids, mask_row, tail, class_ids, norms, g, head, x0, x1, wall, middles, lns, qkvs, atts, probs, hids, slopes):
+    S = jax.ShapeDtypeStruct
+    V = pltpu.VMEM
+    D = pltpu.SemaphoreType.DMA
+    any_ = pl.BlockSpec(memory_space=pl.ANY)
+    vm = pl.BlockSpec(memory_space=pltpu.VMEM)
+    f32, bf = V((ROWS, W), F32), V((ROWS, W), BF)
+    out = pl.pallas_call(
+        backward_kernel,
+        out_shape=(S((4, W, W), BF), S((256, W), F32), S((288, W), F32), S((4, 8, 24, 128), F32), S((24, W, HALF), BF),
+                   S((2, 24, 96, HALF), BF), S((2, 24, 192, HALF), BF), S((24, 96, HALF), BF), S((24, 96, HALF), BF)),
+        in_specs=[pl.BlockSpec(memory_space=pltpu.SMEM)] + [vm] * 5 + [any_] * 12, out_specs=(any_, vm, vm, vm) + (any_,) * 5,
+        scratch_shapes=[f32, f32, f32, bf, bf, V((2, ROWS, W), BF), V((2, ROWS, W), BF), V((3, ROWS, W), BF), V((3, ROWS, W), BF), bf,
+                        V((3, 8, SEQ, SEQ), BF), V((4, W, W), BF), V((4, W, W), BF), V((10, W, HALF), BF),
+                        V((W, HALF), BF), V((2, 96, HALF), BF), V((2, 192, HALF), BF), V((2, 96, HALF), BF), V((24, 192, HALF), BF),
+                        V((16, W), F32), V((1024, HALF), BF), V((3, 256, HALF), BF), V((3, 64, HALF), BF),
+                        V((288, W), F32), V((288, HALF), F32), V((3, 72, HALF), F32), V((4, 72, HALF), F32), V((24, 128), F32),
+                        D((48,)), D((2, 192)), D((8, 4)), D((8, 4)),
+                        D((2,)), D((2,)), D((4,)), D((4,)), D((3,)), D((3,)), D((4,)), D((4,)), D, D, D((3,)), D((3,)), D((4,)), D((4,)), D((4,)), D((4,)),
+                        D((4,)), D((4,)), D((8,)), D((8,))],
+        compiler_params=pltpu.CompilerParams(collective_id=1, has_side_effects=True, vmem_limit_bytes=62 * 2**20),
+        cost_estimate=pl.CostEstimate(flops=24 * 4 * ROWS * W * W, bytes_accessed=150 * 10**6, transcendentals=10**7),
+        name="layers_back",
+    )(block_of, ids, mask_row, tail, class_ids, norms, g, head, x0, x1, wall, middles, lns, qkvs, atts, probs, hids, slopes)
+    return out[:4]
 
 
 def norm_rows(inputs, norm_gain, norm_shift):
@@ -174,6 +913,12 @@
     gradients = jnp.concatenate([grad_qkv, grad_out_proj[None], grad_up, grad_down], axis=0)
     norm_grads = jnp.stack([grad_gain_one, grad_shift_one, grad_gain_two, grad_shift_two])
     return (grad_middle + grad_in_norm, gradients, norm_grads)
+
+
+def pick(blocks, order):
+    return jnp.stack(
+        [lax.dynamic_index_in_dim(blocks, order[i], 0, keepdims=False) for i in range(order.shape[0])]
+    )
 
 
 def on_device(
@@ -214,8 +959,169 @@
     slot_match = slot_of[None, :] == slot_index[:, None]
     filled = jnp.any(slot_match, axis=1)
     block_of = jnp.sum(jnp.where(slot_match, block_index[None, :], 0), axis=1)
+    mask_float = masked.astype(jnp.float32)
+    count = jnp.broadcast_to(jnp.sum(mask_float), (8, 128))
+    classes = jnp.where(dropped == 1, CLASSES, labels)
+    own_rows = images * IMAGE_TOKENS
+    room = ((0, 0), (0, SEQ - IMAGE_TOKENS))
+    kept_ids = jnp.pad(jnp.where(masked == 1, -1, code_ids), room, constant_values=-1).reshape(ROWS, 1)
+    mask_padded = jnp.pad(mask_float, room)
+    positions = jnp.concatenate(
+        [
+            extra_weight[1:seq_len],
+            extra_weight[:1],
+            jnp.zeros((SEQ - REAL, MODEL_WIDTH), jnp.float32),
+        ]
+    )
+    few = jnp.concatenate(
+        [
+            lax.dynamic_index_in_dim(extra_weight, IMAGE_TOKENS + 2 + classes[i], 0, keepdims=True)
+            for i in range(3)
+        ]
+        + [extra_weight[IMAGE_TOKENS + 1][None], jnp.zeros((4, MODEL_WIDTH), jnp.float32)]
+    )
+    norms = jnp.pad(norm_weight, ((0, 6), (0, 0)))
+    all_weights, code_table, masked_total, first, stream1, stream2, *saved = forward(
+        slot_of, chunks_to_send(master_block_weight), embed_weight.astype(BF), count,
+        kept_ids, mask_padded.reshape(ROWS, 1), positions, few, norms,
+    )
+    inverse = 1.0 / masked_total[0, 0]
+    flat_codes = code_ids.reshape(own_rows)
+    code_hot = (flat_codes[:, None] == jnp.arange(CODES)[None, :]).astype(BF)
+    target_rows = jnp.dot(code_hot, code_table, preferred_element_type=jnp.float32)
+    stream = stream2.reshape(images, SEQ, MODEL_WIDTH)[:, :IMAGE_TOKENS].reshape(own_rows, MODEL_WIDTH)
+    final_gain = norm_weight[4 * LAYERS]
+    final_shift = norm_weight[4 * LAYERS + 1]
+    code_final = norm_rows(stream, final_gain, final_shift).astype(BF)
+    flat_mask = mask_float.reshape(own_rows)
+    logits = (
+        jnp.einsum("td,cd->tc", code_final, code_table, preferred_element_type=jnp.float32)
+        + bias_weight
+    )
+    row_top = jnp.max(logits, axis=1)
+    log_total = row_top + jnp.log(jnp.sum(jnp.exp(logits - row_top[:, None]), axis=1))
+    weighted = jnp.exp(logits - log_total[:, None]) * (flat_mask * inverse)[:, None]
+    grad_logits = weighted.astype(jnp.bfloat16)
+    own_weight = flat_mask * inverse
+    target_logit = (
+        jnp.sum(code_final.astype(jnp.float32) * target_rows, axis=1)
+        + jnp.sum(jnp.where(flat_codes[:, None] == jnp.arange(CODES)[None, :], bias_weight, 0.0), axis=1)
+    )
+    loss_part = jnp.sum(own_weight * (log_total - target_logit))
+    grad_code = jnp.dot(grad_logits, code_table, preferred_element_type=jnp.float32)
+    grad_code = grad_code - own_weight[:, None] * target_rows
+    head_table = jnp.einsum(
+        "tc,td->cd", grad_logits, code_final, preferred_element_type=jnp.float32
+    )
+    head_bias = jnp.sum(weighted, axis=0)
+    grad_stream, grad_gain, grad_shift = jax.vjp(norm_rows, stream, final_gain, final_shift)[1](
+        grad_code
+    )
+    grad_stream = jnp.pad(
+        grad_stream.reshape(images, IMAGE_TOKENS, MODEL_WIDTH), ((0, 0), (0, SEQ - IMAGE_TOKENS), (0, 0))
+    ).reshape(ROWS, MODEL_WIDTH)
+    masked_hot = code_hot * flat_mask[:, None].astype(jnp.bfloat16)
+    target_term = jnp.dot(masked_hot.T, code_final, preferred_element_type=jnp.float32)
+    head_term = head_table - inverse * target_term
+    bias_grad = head_bias - inverse * jnp.sum(masked_hot.astype(jnp.float32), axis=0)
+    tail = jnp.concatenate(
+        [
+            jnp.zeros((9, MODEL_WIDTH), jnp.float32),
+            grad_gain[None],
+            grad_shift[None],
+            jnp.pad(bias_grad, (0, 2 * MODEL_WIDTH - CODES)).reshape(2, MODEL_WIDTH),
+            jnp.full((1, MODEL_WIDTH), loss_part),
+            jnp.zeros((2, MODEL_WIDTH), jnp.float32),
+        ]
+    )
+    mask_row = jnp.pad(mask_padded.reshape(1, ROWS), ((0, 15), (0, 0))).astype(BF)
+    class_pack = jnp.pad(classes.astype(jnp.float32)[None], ((0, 7), (0, 125)))
+    owned, table_grad, misc, class_all = backward(
+        block_of, kept_ids, mask_row, tail, class_pack, norms, grad_stream, head_term,
+        first, stream1, all_weights.reshape(BLOCKS, MODEL_WIDTH, MODEL_WIDTH), *saved
+    )
+    owned = owned.astype(jnp.float32)
+    class_rows = class_all[:, :, :18].reshape(-1, MODEL_WIDTH).astype(BF)
+    class_ids = class_all[:, :, 18, :3].reshape(-1) + (seq_len + 1.0)
+    class_hot = (class_ids[:, None] == jnp.arange(extra_weight.shape[0]).astype(jnp.float32)).astype(BF)
+    class_grad = jnp.dot(class_hot.T, class_rows, preferred_element_type=jnp.float32)
+    extra_grad = class_grad + jnp.pad(
+        misc[: seq_len + 1], ((0, extra_weight.shape[0] - seq_len - 1), (0, 0))
+    )
+    norm_grad = misc[265:275]
+    bias_grad = misc[275:277].reshape(-1)[:CODES]
+    step_loss = misc[277, 0]
+    own_filled = lax.dynamic_slice_in_dim(filled, lax.axis_index("dp") * slot_count, slot_count)[
+        :, None, None
+    ]
+    step_float = step_count[0].astype(jnp.float32)
+    block_new = adam_update(
+        master_block_weight, matrix_first_moment, matrix_second_moment, owned, 0.03, step_float
+    )
+    table_new = adam_update(embed_weight, embed_first, embed_second, table_grad, 0.05, step_float)
+    extra_new = adam_update(extra_weight, extra_first, extra_second, extra_grad, 0.5, step_float)
+    norm_new = adam_update(norm_weight, norm_first, norm_second, norm_grad, 0.5, step_float)
+    bias_new = adam_update(bias_weight, bias_first, bias_second, bias_grad, 0.3, step_float)
+    return (
+        step_loss,
+        jnp.where(own_filled, block_new[0], 0.0),
+        jnp.where(own_filled, block_new[1], 0.0),
+        jnp.where(own_filled, block_new[2], 0.0),
+        table_new[0],
+        table_new[1],
+        table_new[2],
+        extra_new[0],
+        extra_new[1],
+        extra_new[2],
+        norm_new[0],
+        norm_new[1],
+        norm_new[2],
+        bias_new[0],
+        bias_new[1],
+        bias_new[2],
+    )
+
+
+def any_mesh(
+    code_ids,
+    masked,
+    labels,
+    dropped,
+    owners,
+    step_count,
+    master_block_weight,
+    matrix_first_moment,
+    matrix_second_moment,
+    embed_weight,
+    embed_first,
+    embed_second,
+    extra_weight,
+    extra_first,
+    extra_second,
+    norm_weight,
+    norm_first,
+    norm_second,
+    bias_weight,
+    bias_first,
+    bias_second,
+):
+    images = code_ids.shape[0]
+    seq_len = IMAGE_TOKENS + 1
+    slot_count = master_block_weight.shape[0]
+    block_count = owners.shape[0]
+    per_layer = BLOCKS // LAYERS
+    block_index = jnp.arange(block_count)
+    same_owner = (owners[None, :] == owners[:, None]) & (
+        block_index[None, :] < block_index[:, None]
+    )
+    owner_rank = jnp.sum(same_owner.astype(jnp.int32), axis=1)
+    slot_of = owners * slot_count + owner_rank
+    slot_index = jnp.arange(slot_count * lax.axis_size("dp"))
+    slot_match = slot_of[None, :] == slot_index[:, None]
+    filled = jnp.any(slot_match, axis=1)
+    block_of = jnp.sum(jnp.where(slot_match, block_index[None, :], 0), axis=1)
     gathered = lax.all_gather(master_block_weight.astype(jnp.bfloat16), "dp", axis=0, tiled=True)
-    all_weights = jnp.take(gathered, slot_of, axis=0)
+    all_weights = pick(gathered, slot_of)
     local_table = embed_weight.astype(jnp.bfloat16)
     code_table = lax.all_gather(local_table, "vocab", axis=0, tiled=True)
     mask_float = masked.astype(jnp.float32)
@@ -347,7 +1253,7 @@
         (loss_part, extra_grad, norm_grad, bias_grad), ("dp", "vocab")
     )
     owned = lax.psum_scatter(
-        jnp.where(filled[:, None, None], jnp.take(all_grads, block_of, axis=0), 0.0).astype(
+        jnp.where(filled[:, None, None], pick(all_grads, block_of), 0.0).astype(
             jnp.bfloat16
         ),
         "dp",
@@ -410,8 +1316,9 @@
         P(),
         P(),
     )
+    fast = mesh.shape["dp"] == 8 and mesh.shape["vocab"] == 4
     return jax.shard_map(
-        on_device,
+        on_device if fast else any_mesh,
         mesh=mesh,
         in_specs=placed,
         out_specs=(

time: 1740 us -> 571 us (0.33)
  waiting for transfers between devices: 557 us -> 0 us
  Pallas kernels: 0 us -> 466 us
  blocking collectives: 455 us -> 0 us
  matrix products: 245 us -> 23.5 us
  local copies, waits for them, and re-layouts: 240 us -> 23.1 us
  other arithmetic: 204 us -> 40 us
    pallas_call x0 -> x2, Pallas kernels: none -> 466 us  [the longest x1 282 us: backward(): pl.pallas_call(backward_kernel, out_shape=(S((4, W, W), BF), S((256, W),...]
    psum x4 -> x0, blocking collectives: 424 us -> none  [the longest x1 322 us: on_device(): owned = lax.psum(owned, 'vocab')]
    reduce_scatter x3 -> x0, waiting for transfers between devices: 304 us -> none  [the longest x1 226 us: on_device(): lax.psum_scatter(jnp.where(filled[:, None, None], jnp.take(all_grads, blo...]
    dot_general x41 -> x5, matrix products: 242 us -> 20.5 us  [the longest x1 8.82 us: on_device(): jnp.dot(class_hot.T, class_rows, preferred_element_type=jnp.float32)]
    all_gather x3 -> x0, waiting for transfers between devices: 219 us -> none  [the longest x1 163 us: on_device(): lax.all_gather(master_block_weight.astype(jnp.bfloat16), 'dp', axis=0, ti...]
    convert_element_type x10 -> x3, other arithmetic: 105 us -> 0.79 us  [the longest x1 0.79 us: on_device(): embed_weight.astype(BF)]
    unnamed x352 -> x50, local copies, waits for them, and re-layouts: 84 us -> 0.44 us
    gather x6 -> x0, local copies, waits for them, and re-layouts: 57 us -> none  [the longest x1 23.5 us: on_device(): jnp.take(all_grads, block_of, axis=0)]
  transfers between devices with their start and end apart: 8 -> 0, of which waited for: 6 -> 0; matrix products, arithmetic and copies ran while one was open for 12% -> 0% of each run, Pallas kernels for 0% -> 0%
where the time goes in v1:
time: 571 us; the launch traced here: 560 us
  Pallas kernels  466 us (82%)
  other arithmetic  40 us (7%)
  matrix products  23.5 us (4%)
  local copies, waits for them, and re-layouts  23.1 us (4%)
  between operations  6.94 us (1%)
    pallas_call x1, Pallas kernels, backward(): pl.pallas_call(backward_kernel, out_shape=(S((4, W, W), BF), S((256, W),...  282 us
    pallas_call x1, Pallas kernels, forward(): pl.pallas_call(forward_kernel, out_shape=shapes, in_specs=[pl.BlockSpec(m...  185 us
    select_n x1, other arithmetic, on_device(): jnp.where(own_filled, block_new[2], 0.0)  24.6 us

profile of v1, /device:TPU:0, one launch (start us, length us, event | category | flops | bytes accessed | tf_op | source)
XLA Modules:
  0.0 559.9 jit_solution(7971314564198152652)
XLA Ops:
  0.7 4.0 fusion.9.send_ref
  9.3 0.8 fusion.32
  10.8 1.2 slice.52
  12.0 1.0 maximum_maximum_fusion.pos_ref
  13.1 1.0 reshape.206.mask_ref
  14.1 1.0 reshape.207.ids_ref
  16.4 0.8 convert_element_type.79.table_ref
  17.8 1.2 broadcast_in_dim.100.count_ref
  19.0 184.5 %layers.1 = (bf16[24,4,2,96,768]{4,3,2,1,0:T(8,128)(2,1)}, bf16[1024,768]{1,0:T(8,128)(2,1)}, f32[8,128]{1,0:T(8,128)}, f32[816,768]{1,0:T(8,128)}, f32[816,768]...) custom-call(s32[24]{0:T(128)} %multiply_add_fusion.5.slot_ref, ...), custom_call_target="tpu_custom_call" | custom-call | flops 23102226432 | bytes 100000000 | tf_op jit(solution)/shard_map/layers/pallas_call | solution.py:397
  203.6 2.1 fusion.33
  206.5 4.6 multiply_reduce_fusion.1
  211.1 1.5 add_reduce_fusion
  212.6 1.8 select_reduce_fusion
  214.5 1.2 slice.61
  217.0 3.0 fusion.10
  220.0 3.4 multiply_subtract_fusion.1.head_ref
  223.4 2.2 multiply_reduce_fusion
  225.6 0.8 fusion.31
  226.7 1.7 pad.39
  228.4 0.7 fusion.7
  229.1 0.7 broadcast_in_dim.105
  229.8 2.0 concatenate.11.tail_ref
  233.7 281.9 %layers_back.1 = (bf16[4,768,768]{2,1,0:T(8,128)(2,1)}, f32[256,768]{1,0:T(8,128)}, f32[288,768]{1,0:T(8,128)}, f32[4,8,24,128]{3,2,1,0:T(8,128)}, bf16[24,768,3...) custom-call(s32[32]{0:T(128)} %select_reduce_fusion.1.block_ref, ...), custom_call_target="tpu_custom_call" | custom-call | flops 46204452864 | bytes 150000000 | tf_op jit(solution)/shard_map/layers_back/pallas_call | solution.py:745
  515.6 1.2 slice.65
  516.8 1.0 slice.82
  518.0 1.0 add_reduce_fusion.1
  519.8 8.8 %multiply_subtract_fusion = (f32[1259,768]{1,0:T(8,128)}, f32[1259,768]{1,0:T(8,128)}, f32[1259,768]{1,0:T(8,128)}) fusion(f32[1259,768]{1,0:T(8,128)} %param.33, f32[]{:T(128)} %bitcast.17, f32[]{:T(128)} %bitcast.16, f32[1259,768]{1,0:T(8,128)} %param.35, f32[1259,768]{1,0:T(8,128)} %param.34, f32[258,768]{1,0:T(8,128)S(1)} %slice.65, ...), kind=kOutput, calls=%fused_computation.11 | convolution fusion | flops 201238560 | bytes 24151348 | tf_op jit(solution)/shard_map/dot_general | solution.py:1047
  528.8 24.6 %fusion.3 = (f32[4,768,768]{2,1,0:T(8,128)}, f32[4,768,768]{2,1,0:T(8,128)}, f32[4,768,768]{2,1,0:T(8,128)}) fusion(bf16[4,768,768]{2,1,0:T(8,128)(2,1)} %get-tuple-element.47, f32[4,768,768]{2,1,0:T(8,128)} %param.29, pred[4]{0:T(512)(128)(4,1)S(1)} %dynamic_slice.21, f32[4,768,768]{2,1,0:T(8,128)} %param.27, f32[]{:T(128)} %bitcast.17, f32[]{:T(128)} %bitcast.16, ...), kind=kLoop, calls=%fused_computation.7 | loop fusion | flops 44826624 | bytes 61341708 | tf_op jit(solution)/shard_map/jit(_where)/select_n | solution.py:1069
  553.5 1.8 multiply_subtract_fusion.3
  555.3 1.6 multiply_subtract_fusion.4
  556.9 0.7 slice.67
  558.3 1.2 slice.62
  (98 shorter events, 8.1 us)
Async XLA Ops:
  0.6 4.1 copy-start.16
  0.7 4.1 copy-start.17
  0.7 12.4 %copy-start.12 = (s32[3,256]{1,0:T(4,128)S(1)}, s32[3,256]{1,0:T(4,128)}, u32[]{:S(2)}) copy-start(s32[3,256]{1,0:T(4,128)} %param.22) | copy-start | bytes 9220
  0.7 12.4 %copy-start.13 = (s32[3,256]{1,0:T(4,128)S(1)}, s32[3,256]{1,0:T(4,128)}, u32[]{:S(2)}) copy-start(s32[3,256]{1,0:T(4,128)} %param.21) | copy-start | bytes 9220
  4.8 10.3 %copy-start.18 = (s32[24]{0:T(128)S(1)}, s32[24]{0:T(128)}, u32[]{:S(2)}) copy-start(s32[24]{0:T(128)} %param.25) | copy-start | bytes 292
  4.8 11.0 %copy-start.8 = (f32[10,768]{1,0:T(8,128)S(1)}, f32[10,768]{1,0:T(8,128)}, u32[]{:S(2)}) copy-start(f32[10,768]{1,0:T(8,128)} %param.36) | copy-start | bytes 92164
  4.8 11.6 %copy-start.3 = (f32[256,768]{1,0:T(8,128)S(1)}, f32[256,768]{1,0:T(8,128)}, u32[]{:S(2)}) copy-start(f32[256,768]{1,0:T(8,128)} %param.30) | copy-start | bytes 2359300
  203.6 2.4 copy-start.2
  205.6 5.4 copy-start
  206.5 4.6 copy-start.11
  206.5 4.6 copy-start.23
  211.1 1.5 copy-start.20
  217.0 3.0 copy-start.21
  220.0 3.4 copy-start.1
  220.0 3.4 copy-start.22
  220.0 3.4 copy-start.24
  226.7 5.8 %copy-start.19 = (s32[24]{0:T(128)S(1)}, s32[24]{0:T(128)}, u32[]{:S(2)}) copy-start(s32[24]{0:T(128)} %multiply_add_fusion.5.slot_ref) | copy-start | bytes 292
  528.8 24.7 %copy-start.4 = (f32[256,768]{1,0:T(8,128)S(1)}, f32[256,768]{1,0:T(8,128)}, u32[]{:S(2)}) copy-start(f32[256,768]{1,0:T(8,128)} %param.30) | copy-start | bytes 2359300
  528.8 24.7 %copy-start.5 = (f32[256,768]{1,0:T(8,128)S(1)}, f32[256,768]{1,0:T(8,128)}, u32[]{:S(2)}) copy-start(f32[256,768]{1,0:T(8,128)} %param.32) | copy-start | bytes 2359300
  528.8 24.7 %copy-start.6 = (f32[256,768]{1,0:T(8,128)S(1)}, f32[256,768]{1,0:T(8,128)}, u32[]{:S(2)}) copy-start(f32[256,768]{1,0:T(8,128)} %param.31) | copy-start | bytes 2359300
  528.8 24.7 %copy-start.7 = (f32[256,768]{1,0:T(8,128)S(1)}, f32[256,768]{1,0:T(8,128)}, u32[]{:S(2)}) copy-start(f32[256,768]{1,0:T(8,128)} %get-tuple-element.48) | copy-start | bytes 2359300
  553.5 1.8 copy-start.9
  553.5 1.8 copy-start.10
  553.5 4.2 copy-start.14
  553.5 4.1 copy-start.15
